TPU v7x, 512 devices: a whole 4x8x8 slice. The times are simulated.
512 devices in a mesh: resp: 32 (over z, x_hi, core), ctx: 16 (over y, x_lo).
Axes of the slice: x: 4 (x_hi: 2, x_lo: 2; x = x_hi * 2 + x_lo), y: 8, z: 8, core: 2. Of those that a mesh axis runs over, the one named last changes fastest.
Arguments:
- query: bfloat16 [32, 2048, 1024], P('resp', 'ctx'), may hold values from -8 to 8
- resp_key: bfloat16 [32, 2048, 128], P('resp', 'ctx'), may hold values from -6 to 6
- resp_value: bfloat16 [32, 2048, 128], P('resp', 'ctx'), may hold values from -6 to 6
- prompt_key: bfloat16 [2048, 128], P('resp'), may hold values from -8 to 8
- prompt_value: bfloat16 [2048, 128], P('resp'), may hold values from -6 to 6
- saved_out: bfloat16 [32, 2048, 1024], P('resp', 'ctx'), may hold values from -6 to 6
- out_grad: bfloat16 [32, 2048, 1024], P('resp', 'ctx'), may hold values from -6 to 6
- resp_len: int32 [32], P('resp'), may hold values from 512 to 2048, as said below
- prompt_order: int32 [32], replicated, may hold values from 0 to 31, each once
Outputs:
- dquery: bfloat16 [32, 2048, 1024], P('resp', 'ctx')
- resp_dkey: bfloat16 [32, 2048, 128], P('resp', 'ctx')
- resp_dvalue: bfloat16 [32, 2048, 128], P('resp', 'ctx')
- prompt_dkey: bfloat16 [2048, 128], P('resp')
- prompt_dvalue: bfloat16 [2048, 128], P('resp')
Inputs may be any that keep to these rules, and one draw needn't show every extreme that they name: A permutation: block j of the stored prompt rows sits at block prompt_order[j] of the prompt. `resp_len`: at least a quarter of each response is not padding; some response has all 2048 tokens.
All inputs are finite; a program needn't handle non-finite values.
Results may differ from a plain program's by a relative error of at most 0.0051.
Values may be sent and summed in bfloat16 or wider, within the bound.
A program may use at most 64 MiB of HBM per device.

v0:
```python
import jax
import jax.numpy as jnp
from jax import lax
from jax.sharding import PartitionSpec as P

HEADS = 8
HEAD_DIM = 128


mask_floor = -1e30


def shifted(block, axis, distance):
    devices = range(lax.axis_size(axis))
    route = [((i - distance) % len(devices), i) for i in devices]
    return lax.ppermute(block, axis, route)


def scores_of(queries, key_rows, score_scale):
    return (
        jnp.einsum("thd,kd->thk", queries, key_rows, preferred_element_type=jnp.float32)
        * score_scale
    )


def update_stats(state_carry, scores, allowed):
    running_max, running_sum = state_carry
    masked = jnp.where(allowed, scores, mask_floor)
    new_max = jnp.maximum(running_max, jnp.max(masked, axis=-1))
    terms = jnp.where(allowed, jnp.exp(masked - new_max[..., None]), 0.0)
    running_sum = running_sum * jnp.exp(running_max - new_max) + jnp.sum(terms, axis=-1)
    return (new_max, running_sum)


def tile_grads(queries, grads_out, log_norm, row_delta, key_rows, value_rows, allowed, score_scale):
    scores = scores_of(queries, key_rows, score_scale)
    probs = jnp.where(allowed, jnp.exp(scores - log_norm[..., None]), 0.0)
    dprobs = jnp.einsum("thd,kd->thk", grads_out, value_rows, preferred_element_type=jnp.float32)
    dscores = probs * (dprobs - row_delta[..., None]) * score_scale
    probs_half = probs.astype(jnp.bfloat16)
    dscores_half = dscores.astype(jnp.bfloat16)
    dquery_tile = jnp.einsum(
        "thk,kd->thd", dscores_half, key_rows, preferred_element_type=jnp.float32
    )
    dkey_tile = jnp.einsum("thk,thd->kd", dscores_half, queries, preferred_element_type=jnp.float32)
    dvalue_tile = jnp.einsum(
        "thk,thd->kd", probs_half, grads_out, preferred_element_type=jnp.float32
    )
    return (dquery_tile, dkey_tile, dvalue_tile)


def local(
    query,
    resp_key,
    resp_value,
    prompt_key,
    prompt_value,
    saved_out,
    out_grad,
    resp_len,
    prompt_order,
):
    tokens = query.shape[1]
    score_scale = HEAD_DIM ** (-0.5)
    queries = query[0].reshape(tokens, HEADS, HEAD_DIM)
    grads_out = out_grad[0].reshape(tokens, HEADS, HEAD_DIM)
    outputs = saved_out[0].reshape(tokens, HEADS, HEAD_DIM)
    row_delta = jnp.sum(grads_out.astype(jnp.float32) * outputs.astype(jnp.float32), axis=-1)
    loop_size = lax.axis_size("ctx")
    ctx_index = lax.axis_index("ctx")
    query_pos = ctx_index * tokens + jnp.arange(tokens, dtype=jnp.int32)
    live_rows = (query_pos < resp_len[0])[:, None, None]

    def causal_mask(begin_row, row_count):
        key_pos = begin_row + jnp.arange(row_count, dtype=jnp.int32)
        return key_pos[None, None, :] <= query_pos[:, None, None]

    block_rows = prompt_key.shape[0]
    prompt_rows = block_rows * lax.axis_size("resp")
    stats_init = (
        jnp.full((tokens, HEADS), mask_floor, jnp.float32),
        jnp.zeros((tokens, HEADS), jnp.float32),
    )
    stats = update_stats(
        stats_init,
        scores_of(queries, lax.all_gather(prompt_key, "resp", axis=0, tiled=True), score_scale),
        True,
    )
    block_keys = lax.all_gather(resp_key[0], "ctx", axis=0, tiled=True)
    scores = scores_of(queries, block_keys, score_scale)
    stats_pair = update_stats(stats, scores, causal_mask(jnp.int32(0), block_keys.shape[0]))
    log_norm = stats_pair[0] + jnp.log(stats_pair[1])
    dquery_tile, dkey_tile, dvalue_tile = tile_grads(
        queries,
        grads_out,
        log_norm,
        row_delta,
        lax.all_gather(prompt_key, "resp", axis=0, tiled=True),
        lax.all_gather(prompt_value, "resp", axis=0, tiled=True),
        live_rows,
        score_scale,
    )
    grad_table = jnp.concatenate([dkey_tile, dvalue_tile], axis=1)
    dquery_sum, grad_table = (dquery_tile, grad_table)
    inverse = jnp.argsort(prompt_order)
    ordered = jnp.take(grad_table.reshape(-1, block_rows, 2 * HEAD_DIM), inverse, axis=0).reshape(
        prompt_rows, 2 * HEAD_DIM
    )
    block_sum = lax.psum_scatter(ordered, "resp", scatter_dimension=0, tiled=True)
    own_prompt = lax.psum(block_sum, "ctx").astype(jnp.bfloat16)
    zero_rows = jnp.zeros((tokens, HEAD_DIM), jnp.float32)

    def loop_turn(rounds, state_carry):
        dquery_part, key_rows, value_rows, dkey_move, dvalue_move = state_carry
        source = (ctx_index - rounds) % loop_size
        allowed = live_rows & causal_mask(source * tokens, tokens)
        dquery_tile, dkey_tile, dvalue_tile = tile_grads(
            queries,
            grads_out,
            log_norm,
            row_delta,
            key_rows.astype(jnp.bfloat16),
            value_rows.astype(jnp.bfloat16),
            allowed,
            score_scale,
        )
        key_rows, value_rows, dkey_move, dvalue_move = shifted(
            (key_rows, value_rows, dkey_move + dkey_tile, dvalue_move + dvalue_tile), "ctx", 1
        )
        return (dquery_part + dquery_tile, key_rows, value_rows, dkey_move, dvalue_move)

    loop_init = (
        dquery_sum,
        resp_key[0].astype(jnp.float32),
        resp_value[0].astype(jnp.float32),
        zero_rows,
        zero_rows,
    )
    dquery_sum, key_back, value_back, dkey_final, dvalue_final = lax.fori_loop(
        0, loop_size, loop_turn, loop_init
    )
    dquery = dquery_sum.reshape(1, tokens, HEADS * HEAD_DIM).astype(jnp.bfloat16)
    resp_dkey = dkey_final.reshape(1, tokens, HEAD_DIM).astype(jnp.bfloat16)
    resp_dvalue = dvalue_final.reshape(1, tokens, HEAD_DIM).astype(jnp.bfloat16)
    prompt_dkey = own_prompt[:, :HEAD_DIM]
    prompt_dvalue = own_prompt[:, HEAD_DIM:]
    return (dquery, resp_dkey, resp_dvalue, prompt_dkey, prompt_dvalue)


def solution(mesh):
    return jax.shard_map(
        local,
        mesh=mesh,
        in_specs=(
            P("resp", "ctx", None),
            P("resp", "ctx", None),
            P("resp", "ctx", None),
            P("resp", None),
            P("resp", None),
            P("resp", "ctx", None),
            P("resp", "ctx", None),
            P("resp"),
            P(),
        ),
        out_specs=(
            P("resp", "ctx", None),
            P("resp", "ctx", None),
            P("resp", "ctx", None),
            P("resp", None),
            P("resp", None),
        ),
        check_vma=False,
    )
```

profile of v0, /device:TPU:4, one launch (start us, length us, event | category | flops | bytes accessed | tf_op | source)
XLA Modules:
  0.0 534.9 jit_solution(14302077783983372224)
XLA Ops:
  11.6 36.6 %all-gather = bf16[1,2048,128]{2,1,0:T(8,128)(2,1)S(1)} all-gather(bf16[1,128,128]{2,1,0:T(8,128)(2,1)S(1)} %copy.58), channel_id=2, replica_groups=mesh['resp'=32,'ctx'=16] {'ctx'}, dimensions={1}, use_global_device_ids=true | all-gather | bytes 557056 | tf_op jit(solution)/shard_map/all_gather | solution.py:89
  48.2 44.9 %all_gather.10 = bf16[2048,128]{1,0:T(8,128)(2,1)S(1)} all-gather(bf16[64,128]{1,0:T(8,128)(2,1)} %param.14), channel_id=1, replica_groups=mesh['resp'=32,'ctx'=16] {'resp'}, dimensions={0}, use_global_device_ids=true | all-gather | bytes 540672 | tf_op jit(solution)/shard_map/all_gather | solution.py:98
  96.1 43.3 %all_gather.12 = bf16[2048,128]{1,0:T(8,128)(2,1)S(1)} all-gather(bf16[64,128]{1,0:T(8,128)(2,1)} %param.15), channel_id=1, replica_groups=mesh['resp'=32,'ctx'=16] {'resp'}, dimensions={0}, use_global_device_ids=true | all-gather | bytes 540672 | tf_op jit(solution)/shard_map/all_gather | solution.py:99
  142.4 4.1 select_reduce_fusion
  163.4 3.4 fusion.31
  167.3 296.8 %while.25 = (s32[]{:T(128)}, f32[128,8,128]{2,0,1:T(8,128)S(1)}, bf16[128,128]{1,0:T(8,128)(2,1)S(1)}, bf16[128,128]{1,0:T(8,128)(2,1)S(1)}, f32[128,128]{1,0:T(...) while((s32[]{:T(128)}, f32[128,8,128]{2,0,1:T(8,128)S(1)}, ...), condition=%wide.region_6.7_spmd.clone.clone, body=%wide.region_5.6_spmd.clone.clone.sunk | while | flops 169017872 | bytes 5778138 | solution.py:139
  194.1 4.9 collective-permute-start.3
  205.1 5.2 collective-permute-start.1
  229.6 3.5 collective-permute-start.2
  237.9 3.8 collective-permute-done.3
  251.2 5.2 collective-permute-start.3
  259.5 3.7 collective-permute-start
  279.7 4.0 collective-permute-start.1
  287.5 4.4 collective-permute-start.3
  298.1 4.2 collective-permute-start.1
  307.3 3.5 collective-permute-start.3
  312.1 4.0 collective-permute-done.3
  318.1 3.5 collective-permute-start.1
  325.4 4.2 collective-permute-start.3
  335.8 4.4 collective-permute-start.1
  344.0 4.3 collective-permute-start.3
  354.4 5.2 collective-permute-start.1
  380.3 4.0 collective-permute-start.3
  390.5 4.3 collective-permute-start.1
  399.1 5.3 collective-permute-start.3
  410.5 4.3 collective-permute-start.1
  428.9 3.5 collective-permute-start.1
  436.2 3.8 collective-permute-start.3
  446.5 4.1 collective-permute-start.1
  455.8 4.0 collective-permute-start.3
  460.5 3.6 collective-permute-done.3
  466.4 61.1 %psum.7 = bf16[64,256]{1,0:T(8,128)(2,1)S(1)} all-reduce(f32[64,256]{1,0:T(8,128)} %reduce-scatter.2.cloned.1.call-done), channel_id=1, replica_groups=mesh['resp'=32,'ctx'=16] {'ctx'}, use_global_device_ids=true, to_apply=%region_9.10 | all-reduce | flops 16384 | bytes 98304 | tf_op jit(solution)/shard_map/psum | solution.py:110
  (322 shorter events, 219.5 us)
Async XLA Ops:
  7.2 459.2 %reduce-scatter.2.cloned.1.call-start = ((), (), s32[]{:S(2)}) async-start(), calls=%async_computation.1 | async-start | bytes 2162688 | tf_op jit(solution)/shard_map/reduce_scatter | solution.py:109
  167.3 11.4 %collective-permute-start = (bf16[128,128]{1,0:T(8,128)(2,1)S(1)}, bf16[128,128]{1,0:T(8,128)(2,1)S(1)}, u32[]{:S(2)}, u32[]{:S(2)}) collective-permute-start(bf16[128,128]{1,0:T(8,128)(2,1)S(1)} %copy.45), channel_id=1, source_target_pairs={{15,0},{0,1},{1,2},{2,3},{3,4},{4,5},{5,6},{6,7},{7,8},{8,9},{9,10... | collective-permute-start | bytes 98312 | tf_op jit(solution)/shard_map/while/body/eval_jaxpr/ppermute | solution.py:16
  184.1 15.1 %collective-permute-start = (bf16[128,128]{1,0:T(8,128)(2,1)S(1)}, bf16[128,128]{1,0:T(8,128)(2,1)S(1)}, u32[]{:S(2)}, u32[]{:S(2)}) collective-permute-start(bf16[128,128]{1,0:T(8,128)(2,1)S(1)} %copy.45), channel_id=1, source_target_pairs={{15,0},{0,1},{1,2},{2,3},{3,4},{4,5},{5,6},{6,7},{7,8},{8,9},{9,10... | collective-permute-start | bytes 98312 | tf_op jit(solution)/shard_map/while/body/eval_jaxpr/ppermute | solution.py:16
  186.0 13.2 %collective-permute-start.1 = (bf16[128,128]{1,0:T(8,128)(2,1)S(1)}, bf16[128,128]{1,0:T(8,128)(2,1)S(1)}, u32[]{:S(2)}, u32[]{:S(2)}) collective-permute-start(bf16[128,128]{1,0:T(8,128)(2,1)S(1)} %copy.46), channel_id=1, source_target_pairs={{15,0},{0,1},{1,2},{2,3},{3,4},{4,5},{5,6},{6,7},{7,8},{8,9},{9,10... | collective-permute-start | bytes 98312 | tf_op jit(solution)/shard_map/while/body/eval_jaxpr/ppermute | solution.py:16
  202.3 15.7 %collective-permute-start = (bf16[128,128]{1,0:T(8,128)(2,1)S(1)}, bf16[128,128]{1,0:T(8,128)(2,1)S(1)}, u32[]{:S(2)}, u32[]{:S(2)}) collective-permute-start(bf16[128,128]{1,0:T(8,128)(2,1)S(1)} %copy.45), channel_id=1, source_target_pairs={{15,0},{0,1},{1,2},{2,3},{3,4},{4,5},{5,6},{6,7},{7,8},{8,9},{9,10... | collective-permute-start | bytes 98312 | tf_op jit(solution)/shard_map/while/body/eval_jaxpr/ppermute | solution.py:16
  205.1 12.9 %collective-permute-start.1 = (bf16[128,128]{1,0:T(8,128)(2,1)S(1)}, bf16[128,128]{1,0:T(8,128)(2,1)S(1)}, u32[]{:S(2)}, u32[]{:S(2)}) collective-permute-start(bf16[128,128]{1,0:T(8,128)(2,1)S(1)} %copy.46), channel_id=1, source_target_pairs={{15,0},{0,1},{1,2},{2,3},{3,4},{4,5},{5,6},{6,7},{7,8},{8,9},{9,10... | collective-permute-start | bytes 98312 | tf_op jit(solution)/shard_map/while/body/eval_jaxpr/ppermute | solution.py:16
  223.2 12.3 %collective-permute-start = (bf16[128,128]{1,0:T(8,128)(2,1)S(1)}, bf16[128,128]{1,0:T(8,128)(2,1)S(1)}, u32[]{:S(2)}, u32[]{:S(2)}) collective-permute-start(bf16[128,128]{1,0:T(8,128)(2,1)S(1)} %copy.45), channel_id=1, source_target_pairs={{15,0},{0,1},{1,2},{2,3},{3,4},{4,5},{5,6},{6,7},{7,8},{8,9},{9,10... | collective-permute-start | bytes 98312 | tf_op jit(solution)/shard_map/while/body/eval_jaxpr/ppermute | solution.py:16
  225.3 10.2 %collective-permute-start.1 = (bf16[128,128]{1,0:T(8,128)(2,1)S(1)}, bf16[128,128]{1,0:T(8,128)(2,1)S(1)}, u32[]{:S(2)}, u32[]{:S(2)}) collective-permute-start(bf16[128,128]{1,0:T(8,128)(2,1)S(1)} %copy.46), channel_id=1, source_target_pairs={{15,0},{0,1},{1,2},{2,3},{3,4},{4,5},{5,6},{6,7},{7,8},{8,9},{9,10... | collective-permute-start | bytes 98312 | tf_op jit(solution)/shard_map/while/body/eval_jaxpr/ppermute | solution.py:16
  241.7 15.0 %collective-permute-start = (bf16[128,128]{1,0:T(8,128)(2,1)S(1)}, bf16[128,128]{1,0:T(8,128)(2,1)S(1)}, u32[]{:S(2)}, u32[]{:S(2)}) collective-permute-start(bf16[128,128]{1,0:T(8,128)(2,1)S(1)} %copy.45), channel_id=1, source_target_pairs={{15,0},{0,1},{1,2},{2,3},{3,4},{4,5},{5,6},{6,7},{7,8},{8,9},{9,10... | collective-permute-start | bytes 98312 | tf_op jit(solution)/shard_map/while/body/eval_jaxpr/ppermute | solution.py:16
  243.6 13.1 %collective-permute-start.1 = (bf16[128,128]{1,0:T(8,128)(2,1)S(1)}, bf16[128,128]{1,0:T(8,128)(2,1)S(1)}, u32[]{:S(2)}, u32[]{:S(2)}) collective-permute-start(bf16[128,128]{1,0:T(8,128)(2,1)S(1)} %copy.46), channel_id=1, source_target_pairs={{15,0},{0,1},{1,2},{2,3},{3,4},{4,5},{5,6},{6,7},{7,8},{8,9},{9,10... | collective-permute-start | bytes 98312 | tf_op jit(solution)/shard_map/while/body/eval_jaxpr/ppermute | solution.py:16
  259.5 13.4 %collective-permute-start = (bf16[128,128]{1,0:T(8,128)(2,1)S(1)}, bf16[128,128]{1,0:T(8,128)(2,1)S(1)}, u32[]{:S(2)}, u32[]{:S(2)}) collective-permute-start(bf16[128,128]{1,0:T(8,128)(2,1)S(1)} %copy.45), channel_id=1, source_target_pairs={{15,0},{0,1},{1,2},{2,3},{3,4},{4,5},{5,6},{6,7},{7,8},{8,9},{9,10... | collective-permute-start | bytes 98312 | tf_op jit(solution)/shard_map/while/body/eval_jaxpr/ppermute | solution.py:16
  263.3 9.6 %collective-permute-start.1 = (bf16[128,128]{1,0:T(8,128)(2,1)S(1)}, bf16[128,128]{1,0:T(8,128)(2,1)S(1)}, u32[]{:S(2)}, u32[]{:S(2)}) collective-permute-start(bf16[128,128]{1,0:T(8,128)(2,1)S(1)} %copy.46), channel_id=1, source_target_pairs={{15,0},{0,1},{1,2},{2,3},{3,4},{4,5},{5,6},{6,7},{7,8},{8,9},{9,10... | collective-permute-start | bytes 98312 | tf_op jit(solution)/shard_map/while/body/eval_jaxpr/ppermute | solution.py:16
  277.8 14.4 %collective-permute-start = (bf16[128,128]{1,0:T(8,128)(2,1)S(1)}, bf16[128,128]{1,0:T(8,128)(2,1)S(1)}, u32[]{:S(2)}, u32[]{:S(2)}) collective-permute-start(bf16[128,128]{1,0:T(8,128)(2,1)S(1)} %copy.45), channel_id=1, source_target_pairs={{15,0},{0,1},{1,2},{2,3},{3,4},{4,5},{5,6},{6,7},{7,8},{8,9},{9,10... | collective-permute-start | bytes 98312 | tf_op jit(solution)/shard_map/while/body/eval_jaxpr/ppermute | solution.py:16
  279.7 12.4 %collective-permute-start.1 = (bf16[128,128]{1,0:T(8,128)(2,1)S(1)}, bf16[128,128]{1,0:T(8,128)(2,1)S(1)}, u32[]{:S(2)}, u32[]{:S(2)}) collective-permute-start(bf16[128,128]{1,0:T(8,128)(2,1)S(1)} %copy.46), channel_id=1, source_target_pairs={{15,0},{0,1},{1,2},{2,3},{3,4},{4,5},{5,6},{6,7},{7,8},{8,9},{9,10... | collective-permute-start | bytes 98312 | tf_op jit(solution)/shard_map/while/body/eval_jaxpr/ppermute | solution.py:16
  295.8 15.3 %collective-permute-start = (bf16[128,128]{1,0:T(8,128)(2,1)S(1)}, bf16[128,128]{1,0:T(8,128)(2,1)S(1)}, u32[]{:S(2)}, u32[]{:S(2)}) collective-permute-start(bf16[128,128]{1,0:T(8,128)(2,1)S(1)} %copy.45), channel_id=1, source_target_pairs={{15,0},{0,1},{1,2},{2,3},{3,4},{4,5},{5,6},{6,7},{7,8},{8,9},{9,10... | collective-permute-start | bytes 98312 | tf_op jit(solution)/shard_map/while/body/eval_jaxpr/ppermute | solution.py:16
  298.1 13.0 %collective-permute-start.1 = (bf16[128,128]{1,0:T(8,128)(2,1)S(1)}, bf16[128,128]{1,0:T(8,128)(2,1)S(1)}, u32[]{:S(2)}, u32[]{:S(2)}) collective-permute-start(bf16[128,128]{1,0:T(8,128)(2,1)S(1)} %copy.46), channel_id=1, source_target_pairs={{15,0},{0,1},{1,2},{2,3},{3,4},{4,5},{5,6},{6,7},{7,8},{8,9},{9,10... | collective-permute-start | bytes 98312 | tf_op jit(solution)/shard_map/while/body/eval_jaxpr/ppermute | solution.py:16
  316.2 13.7 %collective-permute-start = (bf16[128,128]{1,0:T(8,128)(2,1)S(1)}, bf16[128,128]{1,0:T(8,128)(2,1)S(1)}, u32[]{:S(2)}, u32[]{:S(2)}) collective-permute-start(bf16[128,128]{1,0:T(8,128)(2,1)S(1)} %copy.45), channel_id=1, source_target_pairs={{15,0},{0,1},{1,2},{2,3},{3,4},{4,5},{5,6},{6,7},{7,8},{8,9},{9,10... | collective-permute-start | bytes 98312 | tf_op jit(solution)/shard_map/while/body/eval_jaxpr/ppermute | solution.py:16
  318.1 11.8 %collective-permute-start.1 = (bf16[128,128]{1,0:T(8,128)(2,1)S(1)}, bf16[128,128]{1,0:T(8,128)(2,1)S(1)}, u32[]{:S(2)}, u32[]{:S(2)}) collective-permute-start(bf16[128,128]{1,0:T(8,128)(2,1)S(1)} %copy.46), channel_id=1, source_target_pairs={{15,0},{0,1},{1,2},{2,3},{3,4},{4,5},{5,6},{6,7},{7,8},{8,9},{9,10... | collective-permute-start | bytes 98312 | tf_op jit(solution)/shard_map/while/body/eval_jaxpr/ppermute | solution.py:16
  333.7 14.8 %collective-permute-start = (bf16[128,128]{1,0:T(8,128)(2,1)S(1)}, bf16[128,128]{1,0:T(8,128)(2,1)S(1)}, u32[]{:S(2)}, u32[]{:S(2)}) collective-permute-start(bf16[128,128]{1,0:T(8,128)(2,1)S(1)} %copy.45), channel_id=1, source_target_pairs={{15,0},{0,1},{1,2},{2,3},{3,4},{4,5},{5,6},{6,7},{7,8},{8,9},{9,10... | collective-permute-start | bytes 98312 | tf_op jit(solution)/shard_map/while/body/eval_jaxpr/ppermute | solution.py:16
  335.8 12.7 %collective-permute-start.1 = (bf16[128,128]{1,0:T(8,128)(2,1)S(1)}, bf16[128,128]{1,0:T(8,128)(2,1)S(1)}, u32[]{:S(2)}, u32[]{:S(2)}) collective-permute-start(bf16[128,128]{1,0:T(8,128)(2,1)S(1)} %copy.46), channel_id=1, source_target_pairs={{15,0},{0,1},{1,2},{2,3},{3,4},{4,5},{5,6},{6,7},{7,8},{8,9},{9,10... | collective-permute-start | bytes 98312 | tf_op jit(solution)/shard_map/while/body/eval_jaxpr/ppermute | solution.py:16
  352.5 14.1 %collective-permute-start = (bf16[128,128]{1,0:T(8,128)(2,1)S(1)}, bf16[128,128]{1,0:T(8,128)(2,1)S(1)}, u32[]{:S(2)}, u32[]{:S(2)}) collective-permute-start(bf16[128,128]{1,0:T(8,128)(2,1)S(1)} %copy.45), channel_id=1, source_target_pairs={{15,0},{0,1},{1,2},{2,3},{3,4},{4,5},{5,6},{6,7},{7,8},{8,9},{9,10... | collective-permute-start | bytes 98312 | tf_op jit(solution)/shard_map/while/body/eval_jaxpr/ppermute | solution.py:16
  354.4 12.2 %collective-permute-start.1 = (bf16[128,128]{1,0:T(8,128)(2,1)S(1)}, bf16[128,128]{1,0:T(8,128)(2,1)S(1)}, u32[]{:S(2)}, u32[]{:S(2)}) collective-permute-start(bf16[128,128]{1,0:T(8,128)(2,1)S(1)} %copy.46), channel_id=1, source_target_pairs={{15,0},{0,1},{1,2},{2,3},{3,4},{4,5},{5,6},{6,7},{7,8},{8,9},{9,10... | collective-permute-start | bytes 98312 | tf_op jit(solution)/shard_map/while/body/eval_jaxpr/ppermute | solution.py:16
  371.8 12.8 %collective-permute-start = (bf16[128,128]{1,0:T(8,128)(2,1)S(1)}, bf16[128,128]{1,0:T(8,128)(2,1)S(1)}, u32[]{:S(2)}, u32[]{:S(2)}) collective-permute-start(bf16[128,128]{1,0:T(8,128)(2,1)S(1)} %copy.45), channel_id=1, source_target_pairs={{15,0},{0,1},{1,2},{2,3},{3,4},{4,5},{5,6},{6,7},{7,8},{8,9},{9,10... | collective-permute-start | bytes 98312 | tf_op jit(solution)/shard_map/while/body/eval_jaxpr/ppermute | solution.py:16
  373.7 10.9 %collective-permute-start.1 = (bf16[128,128]{1,0:T(8,128)(2,1)S(1)}, bf16[128,128]{1,0:T(8,128)(2,1)S(1)}, u32[]{:S(2)}, u32[]{:S(2)}) collective-permute-start(bf16[128,128]{1,0:T(8,128)(2,1)S(1)} %copy.46), channel_id=1, source_target_pairs={{15,0},{0,1},{1,2},{2,3},{3,4},{4,5},{5,6},{6,7},{7,8},{8,9},{9,10... | collective-permute-start | bytes 98312 | tf_op jit(solution)/shard_map/while/body/eval_jaxpr/ppermute | solution.py:16
  388.6 16.0 %collective-permute-start = (bf16[128,128]{1,0:T(8,128)(2,1)S(1)}, bf16[128,128]{1,0:T(8,128)(2,1)S(1)}, u32[]{:S(2)}, u32[]{:S(2)}) collective-permute-start(bf16[128,128]{1,0:T(8,128)(2,1)S(1)} %copy.45), channel_id=1, source_target_pairs={{15,0},{0,1},{1,2},{2,3},{3,4},{4,5},{5,6},{6,7},{7,8},{8,9},{9,10... | collective-permute-start | bytes 98312 | tf_op jit(solution)/shard_map/while/body/eval_jaxpr/ppermute | solution.py:16
  390.5 14.1 %collective-permute-start.1 = (bf16[128,128]{1,0:T(8,128)(2,1)S(1)}, bf16[128,128]{1,0:T(8,128)(2,1)S(1)}, u32[]{:S(2)}, u32[]{:S(2)}) collective-permute-start(bf16[128,128]{1,0:T(8,128)(2,1)S(1)} %copy.46), channel_id=1, source_target_pairs={{15,0},{0,1},{1,2},{2,3},{3,4},{4,5},{5,6},{6,7},{7,8},{8,9},{9,10... | collective-permute-start | bytes 98312 | tf_op jit(solution)/shard_map/while/body/eval_jaxpr/ppermute | solution.py:16
  407.4 14.5 %collective-permute-start = (bf16[128,128]{1,0:T(8,128)(2,1)S(1)}, bf16[128,128]{1,0:T(8,128)(2,1)S(1)}, u32[]{:S(2)}, u32[]{:S(2)}) collective-permute-start(bf16[128,128]{1,0:T(8,128)(2,1)S(1)} %copy.45), channel_id=1, source_target_pairs={{15,0},{0,1},{1,2},{2,3},{3,4},{4,5},{5,6},{6,7},{7,8},{8,9},{9,10... | collective-permute-start | bytes 98312 | tf_op jit(solution)/shard_map/while/body/eval_jaxpr/ppermute | solution.py:16
  410.5 11.4 %collective-permute-start.1 = (bf16[128,128]{1,0:T(8,128)(2,1)S(1)}, bf16[128,128]{1,0:T(8,128)(2,1)S(1)}, u32[]{:S(2)}, u32[]{:S(2)}) collective-permute-start(bf16[128,128]{1,0:T(8,128)(2,1)S(1)} %copy.46), channel_id=1, source_target_pairs={{15,0},{0,1},{1,2},{2,3},{3,4},{4,5},{5,6},{6,7},{7,8},{8,9},{9,10... | collective-permute-start | bytes 98312 | tf_op jit(solution)/shard_map/while/body/eval_jaxpr/ppermute | solution.py:16
  427.0 13.3 %collective-permute-start = (bf16[128,128]{1,0:T(8,128)(2,1)S(1)}, bf16[128,128]{1,0:T(8,128)(2,1)S(1)}, u32[]{:S(2)}, u32[]{:S(2)}) collective-permute-start(bf16[128,128]{1,0:T(8,128)(2,1)S(1)} %copy.45), channel_id=1, source_target_pairs={{15,0},{0,1},{1,2},{2,3},{3,4},{4,5},{5,6},{6,7},{7,8},{8,9},{9,10... | collective-permute-start | bytes 98312 | tf_op jit(solution)/shard_map/while/body/eval_jaxpr/ppermute | solution.py:16
  428.9 11.4 %collective-permute-start.1 = (bf16[128,128]{1,0:T(8,128)(2,1)S(1)}, bf16[128,128]{1,0:T(8,128)(2,1)S(1)}, u32[]{:S(2)}, u32[]{:S(2)}) collective-permute-start(bf16[128,128]{1,0:T(8,128)(2,1)S(1)} %copy.46), channel_id=1, source_target_pairs={{15,0},{0,1},{1,2},{2,3},{3,4},{4,5},{5,6},{6,7},{7,8},{8,9},{9,10... | collective-permute-start | bytes 98312 | tf_op jit(solution)/shard_map/while/body/eval_jaxpr/ppermute | solution.py:16
  444.5 15.5 %collective-permute-start = (bf16[128,128]{1,0:T(8,128)(2,1)S(1)}, bf16[128,128]{1,0:T(8,128)(2,1)S(1)}, u32[]{:S(2)}, u32[]{:S(2)}) collective-permute-start(bf16[128,128]{1,0:T(8,128)(2,1)S(1)} %copy.45), channel_id=1, source_target_pairs={{15,0},{0,1},{1,2},{2,3},{3,4},{4,5},{5,6},{6,7},{7,8},{8,9},{9,10... | collective-permute-start | bytes 98312 | tf_op jit(solution)/shard_map/while/body/eval_jaxpr/ppermute | solution.py:16
  446.5 13.5 %collective-permute-start.1 = (bf16[128,128]{1,0:T(8,128)(2,1)S(1)}, bf16[128,128]{1,0:T(8,128)(2,1)S(1)}, u32[]{:S(2)}, u32[]{:S(2)}) collective-permute-start(bf16[128,128]{1,0:T(8,128)(2,1)S(1)} %copy.46), channel_id=1, source_target_pairs={{15,0},{0,1},{1,2},{2,3},{3,4},{4,5},{5,6},{6,7},{7,8},{8,9},{9,10... | collective-permute-start | bytes 98312 | tf_op jit(solution)/shard_map/while/body/eval_jaxpr/ppermute | solution.py:16
  (35 other events, 287.5 us)
Sparse Core Ops, SparseCore 0:
  163.6 121.4 reduce-scatter.1
where the time goes:
time: 537 us; the launch traced here: 535 us
  starting transfers between devices  192 us (36%)
  blocking collectives  186 us (35%)
  waiting for transfers between devices  69.2 us (13%)
  matrix products  33 us (6%)
  other arithmetic  24.9 us (5%)
  between operations  14.9 us (3%)
  local copies, waits for them, and re-layouts  12.2 us (2%)
    ppermute x64, starting transfers between devices, shifted(): return lax.ppermute(block, axis, route)  192 us
    ppermute x64, waiting for transfers between devices, shifted(): return lax.ppermute(block, axis, route)  69.2 us
    psum x1, blocking collectives, local(): own_prompt = lax.psum(block_sum, 'ctx').astype(jnp.bfloat16)  61.1 us
    all_gather x1, blocking collectives, local(): lax.all_gather(prompt_key, 'resp', axis=0, tiled=True)  44.9 us
    all_gather x1, blocking collectives, local(): lax.all_gather(prompt_value, 'resp', axis=0, tiled=True)  43.3 us
    all_gather x1, blocking collectives, local(): block_keys = lax.all_gather(resp_key[0], 'ctx', axis=0, tiled=True)  36.6 us
    and x32, other arithmetic, loop_turn(): allowed = live_rows & causal_mask(source * tokens, tokens)  12 us
  transfers between devices with their start and end apart: 65, of which 31 were waited for; matrix products, arithmetic and copies ran while one was open for 7% of the time, Pallas kernels for 0%

commit v1 on v0

v1 whole, which is shorter than its diff:
```python
import math

import jax
import jax.numpy as jnp
from jax import lax
from jax.experimental import pallas as pl
from jax.experimental.pallas import tpu as pltpu
from jax.sharding import PartitionSpec as P

MESH = pl.DeviceIdType.MESH
HEADS = 8
DIM = 128
SCALE = DIM ** (-0.5)
SCALE2 = SCALE * math.log2(math.e)
FLOOR = -1e30
RING = 8
HALF = RING // 2
GROUP = 16
PB = 64
RB = 128
CHUNK = 256
TOKENS = 128
ROWS = TOKENS * HEADS
COLS = ROWS
VMEM = 56 * 1024 * 1024
F32 = jnp.float32
BF16 = jnp.bfloat16


def level_at(s, idx):
    k = (s + 1) // 2
    odd = lax.rem(s, 2)
    return lax.rem(idx + RING + k - 2 * k * odd, RING)


def body(
    q_ref, rk_ref, rv_ref, pk_ref, pv_ref, o_ref, do_ref, len_ref, ord_ref,
    dq_ref, rdk_ref, rdv_ref, pdk_ref, pdv_ref,
    pkv, rkv, qs, dos, qt, dot, delta, pst, gst, mst, m_run, l_run, fac, dqt, inv,
    c1_own, c1_send, c1_recv, c2_send, c2_recv,
    rs_send, rs_recv, ag_send, ag_recv,
    d_own, d_send, d_recv, d_tot, d_xsend, d_xrecv,
    a_rs, a_zs, a_cs, a_xs, b_rs, b_ys, b_xs,
    c1_ss, c1_rs, c2_ss, c2_rs, rs_ss, rs_rs, ag_ss, ag_rs,
    d_ss, d_rs, dx_ss, dx_rs, token,
):
    resp = lax.axis_index("resp")
    ctx = lax.axis_index("ctx")
    z, xh, core = resp // 4, lax.rem(resp // 2, 2), lax.rem(resp, 2)
    y, xl = ctx // 2, lax.rem(ctx, 2)
    z_low = resp - z * 4

    def at_z(step):
        return (lax.rem(z + RING + step, RING) * 4 + z_low, ctx)

    def at_y(step):
        return (resp, lax.rem(y + RING + step, RING) * 2 + xl)

    other_core = (resp + 1 - 2 * core, ctx)
    mirror = (resp + 2 - 4 * xh, ctx + 1 - 2 * xl)
    x_pair = (resp, ctx + 1 - 2 * xl)

    def at_ctx(step):
        return (resp, lax.rem(ctx + step, GROUP))

    def remote(src, dst, ss, rs, device):
        return pltpu.make_async_remote_copy(
            src_ref=src, dst_ref=dst, send_sem=ss, recv_sem=rs,
            device_id=device, device_id_type=MESH,
        )

    barrier = pltpu.get_barrier_semaphore()
    partners = [at_z(1), at_z(-1), at_y(1), at_y(-1), other_core, mirror, x_pair]
    for device in partners:
        pl.semaphore_signal(barrier, inc=1, device_id=device, device_id_type=MESH)

    own_p = resp
    pkv[pl.ds(pl.multiple_of(own_p * PB, PB), PB), 0:DIM] = pk_ref[...]
    pkv[pl.ds(pl.multiple_of(own_p * PB, PB), PB), DIM:] = pv_ref[...]
    rkv[pl.ds(pl.multiple_of(ctx * RB, RB), RB), 0:DIM] = rk_ref[...]
    rkv[pl.ds(pl.multiple_of(ctx * RB, RB), RB), DIM:] = rv_ref[...]
    pl.semaphore_wait(barrier, len(partners))

    def p_block(lev, sub, c):
        return lev * 4 + sub * 2 + c

    def p_slot(b):
        return pkv.at[pl.ds(pl.multiple_of(b * PB, PB), PB)]

    def r_slot(b):
        return rkv.at[pl.ds(pl.multiple_of(b * RB, RB), RB)]

    def a_block(s, own):
        return p_block(level_at(s, z), xh if own else 1 - xh, core)

    def b_block(s, own):
        return level_at(s, y) * 2 + (xl if own else 1 - xl)

    ring_a = (p_slot, a_block, a_rs, a_zs, at_z)
    ring_b = (r_slot, b_block, b_rs, b_ys, at_y)

    def ring_copy(ring, s, own, up):
        slot, block, rs, ss, at = ring
        b = block(s, own)
        return remote(
            slot(b), slot(b), ss.at[s, (0 if own else 2) + (0 if up else 1)], rs.at[b],
            at(1 if up else -1),
        )

    def arrived(ring, b):
        slot, _, rs, ss, at = ring
        remote(slot(b), slot(b), ss.at[0, 0], rs.at[b], at(1)).wait_recv()

    def core_copy(s, own):
        b = a_block(s, own)
        return remote(p_slot(b), p_slot(b), a_cs.at[s, 0 if own else 1], a_rs.at[b], other_core)

    def hops(ring, s, own, act):
        if isinstance(s, int):
            assert s == 0
            act(ring_copy(ring, s, own, True))
            act(ring_copy(ring, s, own, False))
            return
        k = (s + 1) // 2
        odd = lax.rem(s, 2) == 1
        up_limit, down_limit = (HALF, HALF - 1) if own else (HALF - 1, HALF)

        @pl.when(odd & (k < up_limit))
        def _():
            act(ring_copy(ring, s, own, True))

        @pl.when(jnp.logical_not(odd) & (k < down_limit))
        def _():
            act(ring_copy(ring, s, own, False))

    start = lambda copy: copy.start()
    sent = lambda copy: copy.wait_send()

    def ring_step(ring, s, core_too):
        for own in (True, False):
            arrived(ring, ring[1](s, own))
            hops(ring, s, own, start)
            if core_too:
                core_copy(s, own).start()

    a_first = a_block(0, True)
    b_first = b_block(0, True)
    a_mirror = remote(p_slot(a_first), p_slot(a_first), a_xs, a_rs.at[a_first], mirror)
    b_pair = remote(r_slot(b_first), r_slot(b_first), b_xs, b_rs.at[b_first], x_pair)
    a_mirror.start()
    b_pair.start()
    hops(ring_a, 0, True, start)
    hops(ring_b, 0, True, start)
    core_copy(0, True).start()

    for h in range(HEADS):
        lanes = slice(h * DIM, (h + 1) * DIM)
        q = q_ref[:, lanes]
        do = do_ref[:, lanes]
        qs[lanes, :] = q
        dos[lanes, :] = do
        qt[:, lanes] = q.T
        do_t = do.astype(F32).T
        dot[:, lanes] = do_t.astype(BF16)
        delta[:, lanes] = jnp.sum(do_t * o_ref[:, lanes].astype(F32).T, axis=0, keepdims=True)

    m_run[...] = jnp.full_like(m_run, FLOOR)
    l_run[...] = jnp.zeros_like(l_run)
    dqt[...] = jnp.zeros_like(dqt)

    def inverse_of(c, _):
        at = jnp.int32(0)
        for j in range(RING * 4):
            at = jnp.maximum(at, j * (ord_ref[j] == c).astype(jnp.int32))
        inv[c] = at
        return 0

    lax.fori_loop(0, RING * 4, inverse_of, 0)

    arrived(ring_a, a_block(0, False))
    hops(ring_a, 0, False, start)
    core_copy(0, False).start()
    arrived(ring_b, b_block(0, False))
    hops(ring_b, 0, False, start)

    def first_pass(kv, lev, chunk, causal):
        rows = pl.ds(pl.multiple_of(lev * CHUNK, CHUNK), CHUNK)
        blocks = pl.ds(chunk * 4, 4)
        keys = kv[rows, 0:DIM]
        values = kv[rows, DIM:]
        keys_t = keys.T
        for ct in range(ROWS // COLS):
            cols = slice(ct * COLS, (ct + 1) * COLS)
            s = jnp.dot(keys, qt[:, cols], preferred_element_type=F32) * SCALE2
            if causal:
                key_pos = lev * CHUNK + lax.broadcasted_iota(jnp.int32, (CHUNK, COLS), 0)
                lane = lax.broadcasted_iota(jnp.int32, (CHUNK, COLS), 1)
                query_pos = ctx * TOKENS + (lane & (TOKENS - 1))
                s = jnp.where(key_pos <= query_pos, s, FLOOR)
            m_old = m_run[:, cols]
            m_new = jnp.maximum(m_old, jnp.max(s, axis=0, keepdims=True))
            alpha = jnp.exp2(m_old - m_new)
            p = jnp.exp2(s - m_new)
            l_run[:, cols] = l_run[:, cols] * alpha + jnp.sum(p, axis=0, keepdims=True)
            dp = jnp.dot(values, dot[:, cols], preferred_element_type=F32)
            g = (p * (dp - delta[:, cols])).astype(BF16)
            pst[blocks, :, cols] = p.astype(BF16).reshape(4, PB, COLS)
            gst[blocks, :, cols] = g.reshape(4, PB, COLS)
            dq = jnp.dot(keys_t, g, preferred_element_type=F32)
            dqt[:, cols] = dqt[:, cols] * alpha + dq
            m_run[:, cols] = m_new
            mst[chunk, :, cols] = m_new

    def first(s, _):
        @pl.when(s >= 1)
        def _():
            ring_step(ring_a, s, True)

        lev = level_at(s, z)
        arrived(ring_a, p_block(lev, 0, 1 - core))
        arrived(ring_a, p_block(lev, 1, 1 - core))
        first_pass(pkv, lev, lev, False)

        @pl.when(s >= 1)
        def _():
            ring_step(ring_b, s, False)

        r_lev = level_at(s, y)

        @pl.when(r_lev <= y)
        def _():
            first_pass(rkv, r_lev, RING + r_lev, True)

        return 0

    lax.fori_loop(0, RING, first, 0)
    pl.semaphore_signal(token, inc=1, device_id=mirror, device_id_type=MESH)

    lane = lax.broadcasted_iota(jnp.int32, (1, ROWS), 1)
    live = ctx * TOKENS + (lane & (TOKENS - 1)) < len_ref[0]
    m_all = m_run[...]
    inv_l = jnp.where(live, 1.0 / l_run[...], 0.0)
    for i in range(2 * RING):
        factor = jnp.exp2(mst[i] - m_all) * inv_l
        for b in range(4):
            fac[4 * i + b] = factor

    def scaled(store, block):
        return (store[block].astype(F32) * fac[block]).astype(BF16)

    def c1_copy(lev):
        return remote(c1_send.at[lev], c1_recv.at[lev], c1_ss.at[lev], c1_rs.at[lev], other_core)

    def c_term(lev, sub):
        return c1_own[lev, sub] + c1_recv[lev, sub]

    routes = ((4, 2, True, ()), (3, 1, True, ()), (3, 2, False, ()), (2, 2, True, (0, 1)),
              (2, 1, False, ()), (1, 1, True, ()), (1, 1, False, (2, 4)))

    def c_copy(m, up):
        d = 0 if up else 1
        go = routes[m][1]
        return remote(c2_send.at[d, m], c2_recv.at[d, m], c2_ss.at[d, m], c2_rs.at[d, m], at_z(go if up else -go))

    def c_message(m, up):
        d = 0 if up else 1
        dist, _, longer, added = routes[m]
        value = c_term(lax.rem(z + RING + (dist if up else -dist), RING), d if longer else 1 - d)
        for a in added:
            c_copy(a, up).wait_recv()
            value = value + c2_recv[d, a].astype(F32)
        c2_send[d, m] = value.astype(BF16)
        c_copy(m, up).start()

    def c_events(s):
        if s == 6:
            c1_copy(lax.rem(z + HALF, RING)).wait_recv()
            c_message(0, True)
            c_message(0, False)
        plain = {5: (3, True), 4: (3, False), 3: (2, True), 2: (2, False), 1: (1, True), 0: (1, False)}
        if s in plain:
            dist, up = plain[s]
            c1_copy(lax.rem(z + RING + (dist if up else -dist), RING)).wait_recv()
            for m in {3: (1, 2), 2: (4,), 1: (5,)}[dist]:
                c_message(m, up)
        if s == 1:
            c_message(3, True)
            c_message(3, False)
        if s == 0:
            c_message(6, True)
            c_message(6, False)

    def c_total(sub):
        d = sub
        value = c_term(z, sub)
        for m, up in ((3, d == 0), (5, d == 0), (6, d == 1)):
            value = value + c2_recv[0 if up else 1, m].astype(F32)
        return value

    def d_copy(j, kv, up):
        d = 0 if up else 1
        at = at_y(1 if up else -1)
        if j == 1:
            return remote(d_send.at[d, 0, kv, d], d_recv.at[d, 0, kv, d], d_ss.at[d, 0, kv], d_rs.at[d, 0, kv], at)
        return remote(d_send.at[d, j - 1, kv], d_recv.at[d, j - 1, kv], d_ss.at[d, j - 1, kv], d_rs.at[d, j - 1, kv], at)

    def d_step(j):
        dist = HALF + 1 - j
        for kv in range(2):
            for up in (True, False):
                d = 0 if up else 1
                if j > 1:
                    d_copy(j - 1, kv, up).wait_recv()
                lev = lax.rem(y + RING + (dist if up else -dist), RING)
                for sub in range(2):
                    begins = sub == d
                    if j == 1 and not begins:
                        continue
                    value = d_own[lev, kv, sub]
                    if j > 2 or (j == 2 and begins):
                        value = value + d_recv[d, j - 2, kv, sub].astype(F32)
                    d_send[d, j - 1, kv, sub] = value.astype(BF16)
                d_copy(j, kv, up).start()

    def second(i, _):
        s = RING - 1 - i
        lev = level_at(s, z)
        ps, gs = [], []
        for b in range(4):
            stored = inv[lev * 4 + b]
            ps.append(scaled(pst, stored))
            gs.append(scaled(gst, stored))
        dv = jnp.dot(jnp.concatenate(ps, axis=0), dos[...], preferred_element_type=F32)
        dk = jnp.dot(jnp.concatenate(gs, axis=0), qs[...], preferred_element_type=F32) * SCALE
        for sub in range(2):
            for c in range(2):
                rows = slice((sub * 2 + c) * PB, (sub * 2 + c + 1) * PB)

                @pl.when(core == c)
                def _():
                    c1_own[lev, sub, :, 0:DIM] = dk[rows]
                    c1_own[lev, sub, :, DIM:] = dv[rows]

                @pl.when(core != c)
                def _():
                    c1_send[lev, sub, :, 0:DIM] = dk[rows]
                    c1_send[lev, sub, :, DIM:] = dv[rows]

        c1_copy(lev).start()

        r_lev = level_at(s, y)

        @pl.when(r_lev <= y)
        def _():
            first = (RING + r_lev) * 4
            ps = jnp.concatenate([scaled(pst, first + b) for b in range(4)], axis=0)
            gs = jnp.concatenate([scaled(gst, first + b) for b in range(4)], axis=0)
            dv = jnp.dot(ps, dos[...], preferred_element_type=F32)
            dk = jnp.dot(gs, qs[...], preferred_element_type=F32) * SCALE
            for sub in range(2):
                rows = slice(sub * RB, (sub + 1) * RB)
                d_own[r_lev, 0, sub] = dk[rows]
                d_own[r_lev, 1, sub] = dv[rows]

        @pl.when(r_lev > y)
        def _():
            d_own[r_lev] = jnp.zeros((2, 2, RB, DIM), F32)

        for when in range(RING - 1):

            @pl.when(s == when)
            def _():
                c_events(when)

        for j, when in ((1, 7), (2, 3)):

            @pl.when(s == when)
            def _():
                d_step(j)

        return 0

    lax.fori_loop(0, RING, second, 0)

    inv_scaled = inv_l * SCALE
    for h in range(HEADS):
        lanes = slice(h * DIM, (h + 1) * DIM)
        dq_ref[:, lanes] = (dqt[:, lanes] * inv_scaled[:, lanes]).T.astype(BF16)

    d_step(3)

    c1_copy(z).wait_recv()
    for up in (True, False):
        for m in (3, 5, 6):
            c_copy(m, up).wait_recv()
    for sub in range(2):
        value = c_total(sub)
        for i in range(GROUP):
            r, c = i // 2, i % 2
            rs_send[sub, i] = value[r * 8 : (r + 1) * 8, c * DIM : (c + 1) * DIM]

    def rs_copy(dx, step):
        to_xh = xh if dx == 0 else 1 - xh
        to_ctx = lax.rem(ctx + step, GROUP)
        return remote(
            rs_send.at[to_xh, to_ctx], rs_recv.at[dx, step], rs_ss.at[dx, step], rs_rs.at[dx, step],
            (z * 4 + to_xh * 2 + core, to_ctx),
        )

    def ag_copy(step):
        return remote(ag_send, ag_recv.at[ctx], ag_ss.at[step], ag_rs.at[step], at_ctx(step))

    pieces = [(dx, step) for step in range(GROUP) for dx in range(2)][1:]
    pl.semaphore_wait(token, 1)
    for dx, step in pieces:
        rs_copy(dx, step).start()

    d_step(4)

    piece = rs_send[xh, ctx]
    for dx, step in pieces:
        rs_copy(dx, step).wait_recv()
        piece = piece + rs_recv[dx, step]
    ag_send[...] = piece
    ag_recv[ctx] = piece
    for step in range(1, GROUP):
        ag_copy(step).start()

    for kv in range(2):
        for up in (True, False):
            d_copy(HALF, kv, up).wait_recv()
        for sub in range(2):
            d_tot[kv, sub] = d_own[y, kv, sub] + sum(d_recv[d, HALF - 1, kv, sub].astype(F32) for d in range(2))
        d_xsend[kv] = d_tot[kv, 1 - xl].astype(BF16)

    def dx_copy(kv):
        return remote(d_xsend.at[kv], d_xrecv.at[kv], dx_ss.at[kv], dx_rs.at[kv], x_pair)

    for kv in range(2):
        dx_copy(kv).start()
    for kv, out in ((0, rdk_ref), (1, rdv_ref)):
        dx_copy(kv).wait_recv()
        out[...] = (d_tot[kv, xl] + d_xrecv[kv].astype(F32)).astype(BF16)

    for step in range(1, GROUP):
        ag_copy(step).wait_recv()
    for c, out in ((0, pdk_ref), (1, pdv_ref)):
        parts = [ag_recv[2 * r + c] for r in range(GROUP // 2)]
        out[...] = jnp.concatenate(parts, axis=0).astype(BF16)

    a_mirror.wait_send()
    b_pair.wait_send()
    for kv in range(2):
        dx_copy(kv).wait_send()
    for dx, step in pieces:
        rs_copy(dx, step).wait_send()
    for step in range(1, GROUP):
        ag_copy(step).wait_send()
    for up in (True, False):
        for m in range(len(routes)):
            c_copy(m, up).wait_send()
        for j in range(1, HALF + 1):
            for kv in range(2):
                d_copy(j, kv, up).wait_send()
    for own in (True, False):
        hops(ring_a, 0, own, sent)
        hops(ring_b, 0, own, sent)
        core_copy(0, own).wait_send()

    def drain(s, _):
        for own in (True, False):
            hops(ring_a, s, own, sent)
            hops(ring_b, s, own, sent)
            core_copy(s, own).wait_send()
        return 0

    lax.fori_loop(1, RING, drain, 0)

    def drain_c1(s, _):
        c1_copy(s).wait_send()
        return 0

    lax.fori_loop(0, RING, drain_c1, 0)


def hand_over(*refs):
    n = (len(refs) - 1) // 2
    copies = [pltpu.make_async_copy(refs[i], refs[n + i], refs[-1].at[i]) for i in range(n)]
    for copy in copies:
        copy.start()
    for copy in copies:
        copy.wait()


def local(query, resp_key, resp_value, prompt_key, prompt_value, saved_out, out_grad, resp_len, prompt_order):
    vmem = pl.BlockSpec(memory_space=pltpu.VMEM)
    smem = pl.BlockSpec(memory_space=pltpu.SMEM)
    dma = pltpu.SemaphoreType.DMA
    wide = 2 * DIM
    outs = pl.pallas_call(
        body,
        out_shape=(
            jax.ShapeDtypeStruct((TOKENS, HEADS * DIM), BF16),
            jax.ShapeDtypeStruct((RB, DIM), BF16),
            jax.ShapeDtypeStruct((RB, DIM), BF16),
            jax.ShapeDtypeStruct((PB, DIM), BF16),
            jax.ShapeDtypeStruct((PB, DIM), BF16),
        ),
        in_specs=[vmem] * 7 + [smem] * 2,
        out_specs=(vmem,) * 5,
        scratch_shapes=[
            pltpu.VMEM((RING * CHUNK, wide), BF16),
            pltpu.VMEM((RING * CHUNK, wide), BF16),
            pltpu.VMEM((ROWS, DIM), BF16),
            pltpu.VMEM((ROWS, DIM), BF16),
            pltpu.VMEM((DIM, ROWS), BF16),
            pltpu.VMEM((DIM, ROWS), BF16),
            pltpu.VMEM((1, ROWS), F32),
            pltpu.VMEM((2 * RING * 4, PB, ROWS), BF16),
            pltpu.VMEM((2 * RING * 4, PB, ROWS), BF16),
            pltpu.VMEM((2 * RING, 1, ROWS), F32),
            pltpu.VMEM((1, ROWS), F32),
            pltpu.VMEM((1, ROWS), F32),
            pltpu.VMEM((2 * RING * 4, 1, ROWS), F32),
            pltpu.VMEM((DIM, ROWS), F32),
            pltpu.SMEM((RING * 4,), jnp.int32),
            pltpu.VMEM((RING, 2, PB, wide), F32),
            pltpu.VMEM((RING, 2, PB, wide), F32),
            pltpu.VMEM((RING, 2, PB, wide), F32),
            pltpu.VMEM((2, 7, PB, wide), BF16),
            pltpu.VMEM((2, 7, PB, wide), BF16),
            pltpu.VMEM((2, GROUP, 8, DIM), F32),
            pltpu.VMEM((2, GROUP, 8, DIM), F32),
            pltpu.VMEM((8, DIM), F32),
            pltpu.VMEM((GROUP, 8, DIM), F32),
            pltpu.VMEM((RING, 2, 2, RB, DIM), F32),
            pltpu.VMEM((2, HALF, 2, 2, RB, DIM), BF16),
            pltpu.VMEM((2, HALF, 2, 2, RB, DIM), BF16),
            pltpu.VMEM((2, 2, RB, DIM), F32),
            pltpu.VMEM((2, RB, DIM), BF16),
            pltpu.VMEM((2, RB, DIM), BF16),
            dma((RING * 4,)),
            dma((RING, 4)),
            dma((RING, 2)),
            dma,
            dma((GROUP,)),
            dma((RING, 4)),
            dma,
            dma((RING,)),
            dma((RING,)),
            dma((2, 7)),
            dma((2, 7)),
            dma((2, GROUP)),
            dma((2, GROUP)),
            dma((GROUP,)),
            dma((GROUP,)),
            dma((2, HALF, 2)),
            dma((2, HALF, 2)),
            dma((2,)),
            dma((2,)),
            pltpu.SemaphoreType.REGULAR,
        ],
        compiler_params=pltpu.CompilerParams(
            collective_id=0, has_side_effects=True, vmem_limit_bytes=VMEM
        ),
        name="attention_backward",
    )(
        query[0], resp_key[0], resp_value[0], prompt_key, prompt_value,
        saved_out[0], out_grad[0], resp_len, prompt_order,
    )
    anywhere = pl.BlockSpec(memory_space=pl.ANY)
    outs = pl.pallas_call(
        hand_over,
        out_shape=tuple(jax.ShapeDtypeStruct(out.shape, out.dtype) for out in outs),
        in_specs=[anywhere] * 5,
        out_specs=(anywhere,) * 5,
        scratch_shapes=[dma((5,))],
        compiler_params=pltpu.CompilerParams(vmem_limit_bytes=VMEM),
        name="hand_over",
    )(*outs)
    return (outs[0][None], outs[1][None], outs[2][None], outs[3], outs[4])


def solution(mesh):
    token = P("resp", "ctx", None)
    block = P("resp", None)
    return jax.shard_map(
        local,
        mesh=mesh,
        in_specs=(token, token, token, block, block, token, token, P("resp"), P()),
        out_specs=(token, token, token, block, block),
        check_vma=False,
    )
```

time: 537 us -> 82 us (0.15)
  starting transfers between devices: 192 us -> 0 us
  blocking collectives: 186 us -> 0 us
  Pallas kernels: 0 us -> 80.6 us
  waiting for transfers between devices: 69.2 us -> 0 us
  matrix products: 33 us -> 0 us
  other arithmetic: 24.9 us -> 0 us
  between operations: 14.9 us -> 1.29 us
  local copies, waits for them, and re-layouts: 12.2 us -> 0 us
    ppermute x64 -> x0, starting transfers between devices: 192 us -> none  [shifted(): return lax.ppermute(block, axis, route)]
    all_gather x3 -> x0, blocking collectives: 125 us -> none  [the longest x1 44.9 us: local(): lax.all_gather(prompt_key, 'resp', axis=0, tiled=True)]
    pallas_call x0 -> x2, Pallas kernels: none -> 80.6 us  [the longest x1 68.5 us: local(): pl.pallas_call(body, out_shape=(jax.ShapeDtypeStruct((TOKENS, HEADS * DIM...]
    ppermute x64 -> x0, waiting for transfers between devices: 69.2 us -> none  [shifted(): return lax.ppermute(block, axis, route)]
    psum x1 -> x0, blocking collectives: 61.1 us -> none  [local(): own_prompt = lax.psum(block_sum, 'ctx').astype(jnp.bfloat16)]
    dot_general x86 -> x0, matrix products: 33 us -> none  [the longest x17 7.41 us: tile_grads(): jnp.einsum('thd,kd->thk', grads_out, value_rows, preferred_element_type=j...]
    and x33 -> x0, other arithmetic: 12 us -> none  [the longest x32 12 us: loop_turn(): allowed = live_rows & causal_mask(source * tokens, tokens)]
    unnamed x10 -> x0, local copies, waits for them, and re-layouts: 6.4 us -> none
  transfers between devices with their start and end apart: 65 -> 0, of which waited for: 31 -> 0; matrix products, arithmetic and copies ran while one was open for 7% -> 0% of each run, Pallas kernels for 0% -> 0%
where the time goes in v1:
time: 82 us; the launch traced here: 81.9 us
  Pallas kernels  80.6 us (98%)
  between operations  1.29 us (2%)
    pallas_call x1, Pallas kernels, local(): pl.pallas_call(body, out_shape=(jax.ShapeDtypeStruct((TOKENS, HEADS * DIM...  68.5 us
    pallas_call x1, Pallas kernels, local(): pl.pallas_call(hand_over, out_shape=tuple((jax.ShapeDtypeStruct(out.shape...  12.1 us

profile of v1, /device:TPU:4, one launch (start us, length us, event | category | flops | bytes accessed | tf_op | source)
XLA Modules:
  0.0 81.9 jit_solution(10663989973117263976)
XLA Ops:
  1.3 68.5 %attention_backward.1 = (bf16[128,1024]{1,0:T(8,128)(2,1)}, bf16[128,128]{1,0:T(8,128)(2,1)}, bf16[128,128]{1,0:T(8,128)(2,1)}, bf16[64,128]{1,0:T(8,128)(2,1)}, bf16[64,128]{1,0:T(8,128)(2,1)}) custom-call(bf16[128,1024]{1,0:T(8,128)(2,1)} %bitcast.8, bf16[128,128]{1,0:T(8,128)(2,1)} %bitcast.11, bf16[128,128]{1,0:T(8,128)(2,1)} %bitcast.12, ...), custom_call_target="tpu_custom_call" | custom-call | tf_op jit(solution)/shard_map/attention_backward/pallas_call | solution.py:500
  69.8 12.1 %hand_over.1 = (bf16[128,1024]{1,0:T(8,128)(2,1)}, bf16[128,128]{1,0:T(8,128)(2,1)}, bf16[128,128]{1,0:T(8,128)(2,1)}, bf16[64,128]{1,0:T(8,128)(2,1)}, bf16[64,128]{1,0:T(8,128)(2,1)}) custom-call(bf16[128,1024]{1,0:T(8,128)(2,1)} %get-tuple-element.15.refs_0_, bf16[128,128]{1,0:T(8,128)(2,1)} %get-tuple-element.16.refs_1_, ...), custom_call_target="tpu_custom_call" | custom-call | tf_op jit(solution)/shard_map/hand_over/pallas_call | solution.py:572

commit v2 on v1

v2 whole, which is shorter than its diff:
```python
import math

import jax
import jax.numpy as jnp
from jax import lax
from jax.experimental import pallas as pl
from jax.experimental.pallas import tpu as pltpu
from jax.sharding import PartitionSpec as P

MESH = pl.DeviceIdType.MESH
HEADS = 8
DIM = 128
SCALE = DIM ** (-0.5)
SCALE2 = SCALE * math.log2(math.e)
FLOOR = -1e30
RING = 8
HALF = RING // 2
GROUP = 16
PB = 64
RB = 128
CHUNK = 256
TOKENS = 128
ROWS = TOKENS * HEADS
VMEM = 56 * 1024 * 1024
F32 = jnp.float32
BF16 = jnp.bfloat16


def level_at(s, idx):
    k = (s + 1) // 2
    odd = lax.rem(s, 2)
    return lax.rem(idx + RING + k - 2 * k * odd, RING)


def body(
    q_hbm, rk_hbm, rv_hbm, pk_hbm, pv_hbm, o_hbm, do_hbm, len_ref, order_ref,
    dq_ref, rdk_ref, rdv_ref, pdk_ref, pdv_ref,
    q_ref, o_ref, do_ref, pkv, rkeys, rvalues, qs, dos, qt, dot, delta, pst, gst, mst, m_run, m_dq, l_run, fac, dqt, dqr, inv_v, inv,
    c1_own, c1_send, c1_recv, c2_send, c2_recv,
    rs_send, rs_recv, ag_recv,
    d_own, d_send, d_recv, d_tot, d_xsend, d_xrecv,
    in_s, inv_s, a_rs, a_cr, a_ss, bk_rs, bk_ss, bv_rs, bv_ss,
    c1_ss, c1_rs, c2_ss, c2_rs, rs_ss, rs_rs, ag_ss, ag_rs,
    d_ss, d_rs, dx_ss, dx_rs, token,
):
    resp = lax.axis_index("resp")
    ctx = lax.axis_index("ctx")
    z, xh, core = resp // 4, lax.rem(resp // 2, 2), lax.rem(resp, 2)
    y, xl = ctx // 2, lax.rem(ctx, 2)
    z_low = resp - z * 4

    def at_z(step, across=False):
        low, c = (z_low + 2 - 4 * xh, ctx + 1 - 2 * xl) if across else (z_low, ctx)
        return (lax.rem(z + RING + step, RING) * 4 + low, c)

    def at_y(step, across=False):
        return (resp, lax.rem(y + RING + step, RING) * 2 + (1 - xl if across else xl))

    other_core = (resp + 1 - 2 * core, ctx)
    mirror = (resp + 2 - 4 * xh, ctx + 1 - 2 * xl)
    x_pair = (resp, ctx + 1 - 2 * xl)

    def at_ctx(step):
        return (resp, lax.rem(ctx + step, GROUP))

    def remote(src, dst, ss, rs, device):
        return pltpu.make_async_remote_copy(
            src_ref=src, dst_ref=dst, send_sem=ss, recv_sem=rs,
            device_id=device, device_id_type=MESH,
        )

    barrier = pltpu.get_barrier_semaphore()
    partners = [other_core, mirror, x_pair]
    partners += [at(step, across) for at in (at_z, at_y) for step in (1, -1) for across in (False, True)]
    for device in partners:
        pl.semaphore_signal(barrier, inc=1, device_id=device, device_id_type=MESH)

    p_rows = pl.ds(pl.multiple_of(resp * PB, PB), PB)
    r_rows = pl.ds(pl.multiple_of(ctx * RB, RB), RB)
    moves = (
        (pk_hbm, pkv.at[p_rows, 0:DIM]), (pv_hbm, pkv.at[p_rows, DIM : 2 * DIM]),
        (rk_hbm, rkeys.at[r_rows]), (rv_hbm, rvalues.at[r_rows]),
        (q_hbm, q_ref), (do_hbm, do_ref), (o_hbm, o_ref),
    )
    reads = [pltpu.make_async_copy(src, dst, in_s.at[i]) for i, (src, dst) in enumerate(moves)]
    for read in reads:
        read.start()
    for read in reads[:4]:
        read.wait()
    pl.semaphore_wait(barrier, len(partners))

    def p_block(lev, sub, c):
        return lev * 4 + sub * 2 + c

    def p_slot(b):
        return pkv.at[pl.ds(pl.multiple_of(b * PB, PB), PB)]

    def r_slot(buffer):
        return lambda b: buffer.at[pl.ds(pl.multiple_of(b * RB, RB), RB)]

    def a_block(s, own):
        return p_block(level_at(s, z), xh if own else 1 - xh, core)

    def b_block(s, own):
        return level_at(s, y) * 2 + (xl if own else 1 - xl)

    ring_a = (p_slot, a_block, lambda b: a_rs.at[b // 2], a_ss, at_z)
    ring_k = (r_slot(rkeys), b_block, lambda b: bk_rs.at[b], bk_ss, at_y)
    ring_v = (r_slot(rvalues), b_block, lambda b: bv_rs.at[b], bv_ss, at_y)

    def ring_copy(ring, s, own, device):
        slot, block, rs, ss, _ = ring
        b = block(s, own)
        return remote(slot(b), slot(b), ss, rs(b), device)

    def arrived(ring, b):
        slot, _, rs, ss, at = ring
        remote(slot(b), slot(b), ss, rs(b), at(1)).wait_recv()

    def core_copy(s, own):
        b = a_block(s, own)
        return remote(p_slot(b), p_slot(b), a_ss, a_cr.at[b // 4], other_core)

    def core_arrived(lev):
        both = pkv.at[pl.ds(pl.multiple_of(lev * CHUNK, CHUNK), 2 * PB)]
        remote(both, both, a_ss, a_cr.at[lev], other_core).wait_recv()

    def all_sent(ref, ss):
        remote(ref, ref, ss, dx_rs.at[0], other_core).wait_send()

    def hops(ring, s, own):
        k = (s + 1) // 2
        odd = lax.rem(s, 2) == 1
        up_limit, down_limit = (HALF, HALF - 1) if own else (HALF - 1, HALF)

        @pl.when(odd & (k < up_limit))
        def _():
            ring_copy(ring, s, own, ring[4](1)).start()

        @pl.when(jnp.logical_not(odd) & (k < down_limit))
        def _():
            ring_copy(ring, s, own, ring[4](-1)).start()

    def ring_step(ring, s, core_too):
        for own in (True, False):
            arrived(ring, ring[1](s, own))
            hops(ring, s, own)
            if core_too:
                core_copy(s, own).start()

    def first_copies(ring, pair):
        for step in (1, -1):
            for across in (False, True):
                ring_copy(ring, 0, True, ring[4](step, across)).start()
        ring_copy(ring, 0, True, pair).start()

    first_copies(ring_a, mirror)
    core_copy(0, True).start()
    first_copies(ring_k, x_pair)
    first_copies(ring_v, x_pair)

    def prepare(h):
        lanes = slice(h * DIM, (h + 1) * DIM)
        q = q_ref[:, lanes]
        do = do_ref[:, lanes]
        qs[lanes, :] = q
        dos[lanes, :] = do
        qt[:, lanes] = q.T
        dot[:, lanes] = do.T
        product = do.astype(F32) * o_ref[:, lanes].astype(F32)
        delta[:, lanes] = jnp.sum(product.T, axis=0, keepdims=True)

    for read in reads[4:]:
        read.wait()
    for h in range(HEADS):
        prepare(h)
    arrived(ring_a, a_block(0, False))
    core_copy(0, False).start()
    arrived(ring_k, b_block(0, False))

    m_run[...] = jnp.full_like(m_run, FLOOR)
    m_dq[...] = jnp.full_like(m_dq, FLOOR)
    l_run[...] = jnp.zeros_like(l_run)
    dqt[...] = jnp.zeros_like(dqt)
    dqr[...] = jnp.zeros_like(dqr)

    places = lax.broadcasted_iota(jnp.int32, (RING * 4, RING * 4), 0)
    stored_at = lax.broadcasted_iota(jnp.int32, (RING * 4, RING * 4), 1)
    found = jnp.max(jnp.where(order_ref[...] == places, stored_at, 0), axis=1, keepdims=True)
    inv_v[:, 0 : RING * 4] = jnp.max(jnp.where(places == stored_at, found, 0), axis=0, keepdims=True)
    inv_copy = pltpu.make_async_copy(inv_v, inv, inv_s)
    inv_copy.start()

    def weights(keys, chunk, key_start):
        s = jnp.dot(keys, qt[...], preferred_element_type=F32) * SCALE2
        if key_start is not None:
            key_pos = key_start + lax.broadcasted_iota(jnp.int32, (CHUNK, ROWS), 0)
            lane = lax.broadcasted_iota(jnp.int32, (CHUNK, ROWS), 1)
            s = jnp.where(key_pos <= ctx * TOKENS + (lane & (TOKENS - 1)), s, FLOOR)
        m_old = m_run[...]
        m_new = jnp.maximum(m_old, jnp.max(s, axis=0, keepdims=True))
        alpha = jnp.exp2(m_old - m_new)
        p = jnp.exp2(s - m_new)
        l_run[...] = l_run[...] * alpha + jnp.sum(p, axis=0, keepdims=True)
        m_run[...] = m_new
        mst[chunk] = m_new
        pst[pl.ds(chunk * 4, 4)] = p.reshape(4, PB, ROWS)
        return p, m_new

    def level_rows(lev):
        return pl.ds(pl.multiple_of(lev * CHUNK, CHUNK), CHUNK)

    def prompt_first(lev):
        keys = pkv[level_rows(lev), 0:DIM]
        p, m_new = weights(keys, lev, None)
        alpha = jnp.exp2(m_dq[...] - m_new)
        m_dq[...] = m_new
        dp = jnp.dot(pkv[level_rows(lev), DIM:], dot[...], preferred_element_type=F32)
        g = p * (dp - delta[...])
        gst[pl.ds(lev * 4, 4)] = g.reshape(4, PB, ROWS)
        dqt[...] = dqt[...] * alpha + jnp.dot(keys.T, g.astype(BF16), preferred_element_type=F32)

    def both_sides(k, then):
        for side in range(2):
            s = 2 * k - 1 + side

            @pl.when((s >= 1) & (s < RING))
            def _():
                then(s)

    def first(k, _):
        both_sides(k, lambda s: ring_step(ring_a, s, True))
        both_sides(k, lambda s: ring_step(ring_k, s, False))

        def prompt_side(s, _):
            @pl.when((s >= 0) & (s < RING))
            def _():
                lev = level_at(s, z)
                core_arrived(lev)
                prompt_first(lev)

            return 0

        lax.fori_loop(2 * k - 1, 2 * k + 1, prompt_side, 0)
        both_sides(k - 1, lambda s: ring_step(ring_v, s, False))

        def resp_side(s, _):
            lev = level_at(s, y)

            @pl.when((s >= 0) & (s < RING) & (lev <= y))
            def _():
                weights(rkeys[level_rows(lev), :], RING + lev, lev * CHUNK)

            return 0

        lax.fori_loop(2 * k - 1, 2 * k + 1, resp_side, 0)

        return 0

    lax.fori_loop(0, HALF + 1, first, 0)
    inv_copy.wait()
    pl.semaphore_signal(token, inc=1, device_id=mirror, device_id_type=MESH)

    lane = lax.broadcasted_iota(jnp.int32, (1, ROWS), 1)
    live = ctx * TOKENS + (lane & (TOKENS - 1)) < len_ref[0]
    m_all = m_run[...]
    inv_l = jnp.where(live, 1.0 / l_run[...], 0.0)
    for i in range(2 * RING):
        factor = jnp.exp2(mst[i] - m_all) * inv_l
        for b in range(4):
            fac[4 * i + b] = factor

    def scaled(store, block):
        return (store[block] * fac[block]).astype(BF16)

    def c1_copy(lev):
        return remote(c1_send.at[lev], c1_recv.at[lev], c1_ss, c1_rs.at[lev], other_core)

    def c_term(lev, sub):
        return c1_own[lev, sub] + c1_recv[lev, sub]

    routes = ((4, 2, True, ()), (3, 1, True, ()), (3, 2, False, ()), (2, 2, True, (0, 1)),
              (2, 1, False, ()), (1, 1, True, ()), (1, 1, False, (2, 4)))

    def c_copy(m, up):
        d = 0 if up else 1
        go = routes[m][1]
        return remote(c2_send.at[d, m], c2_recv.at[d, m], c2_ss, c2_rs.at[d, m], at_z(go if up else -go))

    def c_message(m, up):
        d = 0 if up else 1
        dist, _, longer, added = routes[m]
        value = c_term(lax.rem(z + RING + (dist if up else -dist), RING), d if longer else 1 - d)
        for a in added:
            c_copy(a, up).wait_recv()
            value = value + c2_recv[d, a].astype(F32)
        c2_send[d, m] = value.astype(BF16)
        c_copy(m, up).start()

    def c_events(s):
        if s == 6:
            c1_copy(lax.rem(z + HALF, RING)).wait_recv()
            c_message(0, True)
            c_message(0, False)
        plain = {5: (3, True), 4: (3, False), 3: (2, True), 2: (2, False), 1: (1, True), 0: (1, False)}
        if s in plain:
            dist, up = plain[s]
            c1_copy(lax.rem(z + RING + (dist if up else -dist), RING)).wait_recv()
            for m in {3: (1, 2), 2: (4,), 1: (5,)}[dist]:
                c_message(m, up)

    def c_total(sub):
        d = sub
        value = c_term(z, sub)
        for m, up in ((3, d == 0), (5, d == 0), (6, d == 1)):
            value = value + c2_recv[0 if up else 1, m].astype(F32)
        return value

    holds = lax.rem(y, 2) == xl

    def rs_copy(dx, step):
        to_xh = xh if dx == 0 else 1 - xh
        to_y = lax.rem(y + step, RING)
        return remote(
            rs_send.at[to_xh, to_y], rs_recv.at[(dx * RING + step) * 2 + xl], rs_ss, rs_rs,
            (z * 4 + to_xh * 2 + core, 2 * to_y + lax.rem(to_y, 2)),
        )

    def ag_copy(step):
        return remote(ag_recv.at[y], ag_recv.at[y], ag_ss, ag_rs, at_ctx(step))

    far_first = (4, 3, 5, 2, 6, 1, 7, 0)

    def c_scatter():
        c1_copy(z).wait_recv()
        for up in (True, False):
            for m in (3, 5, 6):
                c_copy(m, up).wait_recv()
        for sub in range(2):
            value = c_total(sub).astype(BF16)
            for i in range(RING):
                r, c = i // 2, i % 2
                rs_send[sub, i] = value[r * 16 : (r + 1) * 16, c * DIM : (c + 1) * DIM]
        pl.semaphore_wait(token, 1)
        for step in far_first[:-1]:
            rs_copy(1, step).start()
            rs_copy(0, step).start()
        rs_copy(1, 0).start()

        @pl.when(holds)
        def _():
            rs_recv[xl] = rs_send[xh, y]

        @pl.when(jnp.logical_not(holds))
        def _():
            rs_copy(0, 0).start()

    def c_gather():
        @pl.when(holds)
        def _():
            rest = rs_recv.at[0 : 4 * RING - 1]
            remote(rest, rest, rs_ss, rs_rs, other_core).wait_recv()
            piece = rs_recv[0].astype(F32)
            for i in range(1, 4 * RING):
                piece = piece + rs_recv[i].astype(F32)
            ag_recv[y] = piece.astype(BF16)
            for step in (8, 7, 9, 6, 10, 5, 11, 4, 12, 3, 13, 2, 14, 1, 15):
                ag_copy(step).start()

    def c_finish():
        @pl.when(holds)
        def _():
            rest = ag_recv.at[0 : RING - 1]
            remote(rest, rest, ag_ss, ag_rs, other_core).wait_recv()

        @pl.when(jnp.logical_not(holds))
        def _():
            remote(ag_recv, ag_recv, ag_ss, ag_rs, other_core).wait_recv()

        for c, out in ((0, pdk_ref), (1, pdv_ref)):
            for r in range(RING // 2):
                out[r * 16 : (r + 1) * 16, :] = ag_recv[2 * r + c]

    def d_copy(j, kv, up):
        d = 0 if up else 1
        at = at_y(1 if up else -1)
        if j == 1:
            return remote(d_send.at[d, 0, kv, d], d_recv.at[d, 0, kv, d], d_ss.at[0], d_rs.at[d, 0, kv], at)
        return remote(d_send.at[d, j - 1, kv], d_recv.at[d, j - 1, kv], d_ss.at[1], d_rs.at[d, j - 1, kv], at)

    def d_step(j):
        dist = HALF + 1 - j
        for kv in range(2):
            for up in (True, False):
                d = 0 if up else 1
                if j > 1:
                    d_copy(j - 1, kv, up).wait_recv()
                lev = lax.rem(y + RING + (dist if up else -dist), RING)
                for sub in range(2):
                    begins = sub == d
                    if j == 1 and not begins:
                        continue
                    value = d_own[lev, kv, sub]
                    if j > 2 or (j == 2 and begins):
                        value = value + d_recv[d, j - 2, kv, sub].astype(F32)
                    d_send[d, j - 1, kv, sub] = value.astype(BF16)
                d_copy(j, kv, up).start()

    def prompt_second(i, _):
        s = RING - 1 - i
        lev = level_at(s, z)
        ps, gs = [], []
        for b in range(4):
            stored = inv[0, lev * 4 + b]
            ps.append(scaled(pst, stored))
            gs.append(scaled(gst, stored))
        dv = jnp.dot(jnp.concatenate(ps, axis=0), dos[...], preferred_element_type=F32)
        dk = jnp.dot(jnp.concatenate(gs, axis=0), qs[...], preferred_element_type=F32) * SCALE
        for sub in range(2):
            for c in range(2):
                rows = slice((sub * 2 + c) * PB, (sub * 2 + c + 1) * PB)

                @pl.when(core == c)
                def _():
                    c1_own[lev, sub, :, 0:DIM] = dk[rows]
                    c1_own[lev, sub, :, DIM:] = dv[rows]

                @pl.when(core != c)
                def _():
                    c1_send[lev, sub, :, 0:DIM] = dk[rows]
                    c1_send[lev, sub, :, DIM:] = dv[rows]

        c1_copy(lev).start()

        for when in range(RING - 1):

            @pl.when(s == when)
            def _():
                c_events(when)

        return 0

    lax.fori_loop(0, RING, prompt_second, 0)
    arrived(ring_v, b_block(0, False))
    ring_step(ring_v, jnp.int32(RING - 1), False)

    def resp_second(i, _):
        s = RING - 1 - i
        lev = level_at(s, y)

        @pl.when(lev <= y)
        def _():
            keys = rkeys[level_rows(lev), :]
            dp = jnp.dot(rvalues[level_rows(lev), :], dot[...], preferred_element_type=F32)
            block = (RING + lev) * 4
            p = pst[pl.ds(block, 4)].reshape(CHUNK, ROWS) * fac[block]
            g = (p * (dp - delta[...])).astype(BF16)
            dv = jnp.dot(p.astype(BF16), dos[...], preferred_element_type=F32)
            dk = jnp.dot(g, qs[...], preferred_element_type=F32) * SCALE
            dqr[...] += jnp.dot(keys.T, g, preferred_element_type=F32)
            for sub in range(2):
                rows = slice(sub * RB, (sub + 1) * RB)
                d_own[lev, 0, sub] = dk[rows]
                d_own[lev, 1, sub] = dv[rows]

        @pl.when(lev > y)
        def _():
            d_own[lev] = jnp.zeros((2, 2, RB, DIM), F32)

        @pl.when(s == 7)
        def _():
            d_step(1)
            c_message(3, True)
            c_message(3, False)

        @pl.when(s == 6)
        def _():
            c_message(6, True)
            c_message(6, False)

        @pl.when(s == 3)
        def _():
            c_scatter()
            d_step(2)

        return 0

    lax.fori_loop(0, RING, resp_second, 0)

    dq_factor = jnp.exp2(m_dq[...] - m_all) * inv_l
    for h in range(HEADS):
        lanes = slice(h * DIM, (h + 1) * DIM)
        dq = dqt[:, lanes] * dq_factor[:, lanes] + dqr[:, lanes]
        dq_ref[:, lanes] = (dq * SCALE).T.astype(BF16)

    d_step(3)

    c_gather()
    d_step(4)

    for kv in range(2):
        for up in (True, False):
            d_copy(HALF, kv, up).wait_recv()
        for sub in range(2):
            d_tot[kv, sub] = d_own[y, kv, sub] + sum(d_recv[d, HALF - 1, kv, sub].astype(F32) for d in range(2))
        d_xsend[kv] = d_tot[kv, 1 - xl].astype(BF16)

    def dx_copy(kv):
        return remote(d_xsend.at[kv], d_xrecv.at[kv], dx_ss, dx_rs.at[kv], x_pair)

    for kv in range(2):
        dx_copy(kv).start()
    for kv, out in ((0, rdk_ref), (1, rdv_ref)):
        dx_copy(kv).wait_recv()
        out[...] = (d_tot[kv, xl] + d_xrecv[kv].astype(F32)).astype(BF16)

    c_finish()

    all_sent(pkv.at[0 : 31 * PB], a_ss)
    all_sent(rkeys.at[0 : 15 * RB], bk_ss)
    all_sent(rvalues.at[0 : 15 * RB], bv_ss)
    all_sent(c1_send, c1_ss)
    all_sent(c2_send, c2_ss)
    all_sent(d_send.at[0, 0], d_ss.at[0])
    all_sent(d_send.at[:, 1:HALF], d_ss.at[1])
    all_sent(d_xsend, dx_ss)

    @pl.when(holds)
    def _():
        all_sent(rs_recv.at[0:15], rs_ss)
        all_sent(rs_recv.at[0:15], ag_ss)

    @pl.when(jnp.logical_not(holds))
    def _():
        all_sent(rs_recv.at[0:16], rs_ss)


def hand_over(*refs):
    n = len(refs) // 2
    for i in range(n):
        refs[n + i][...] = refs[i][...]


def local(query, resp_key, resp_value, prompt_key, prompt_value, saved_out, out_grad, resp_len, prompt_order):
    vmem = pl.BlockSpec(memory_space=pltpu.VMEM)
    smem = pl.BlockSpec(memory_space=pltpu.SMEM)
    dma = pltpu.SemaphoreType.DMA
    wide = 2 * DIM
    outs = pl.pallas_call(
        body,
        out_shape=(
            jax.ShapeDtypeStruct((TOKENS, HEADS * DIM), BF16),
            jax.ShapeDtypeStruct((RB, DIM), BF16),
            jax.ShapeDtypeStruct((RB, DIM), BF16),
            jax.ShapeDtypeStruct((PB, DIM), BF16),
            jax.ShapeDtypeStruct((PB, DIM), BF16),
        ),
        in_specs=[pl.BlockSpec(memory_space=pl.ANY)] * 7 + [smem, vmem],
        out_specs=(vmem,) * 5,
        scratch_shapes=[
            pltpu.VMEM((TOKENS, ROWS), BF16),
            pltpu.VMEM((TOKENS, ROWS), BF16),
            pltpu.VMEM((TOKENS, ROWS), BF16),
            pltpu.VMEM((RING * CHUNK, wide), BF16),
            pltpu.VMEM((RING * CHUNK, DIM), BF16),
            pltpu.VMEM((RING * CHUNK, DIM), BF16),
            pltpu.VMEM((ROWS, DIM), BF16),
            pltpu.VMEM((ROWS, DIM), BF16),
            pltpu.VMEM((DIM, ROWS), BF16),
            pltpu.VMEM((DIM, ROWS), BF16),
            pltpu.VMEM((1, ROWS), F32),
            pltpu.VMEM((2 * RING * 4, PB, ROWS), F32),
            pltpu.VMEM((RING * 4, PB, ROWS), F32),
            pltpu.VMEM((2 * RING, 1, ROWS), F32),
            pltpu.VMEM((1, ROWS), F32),
            pltpu.VMEM((1, ROWS), F32),
            pltpu.VMEM((1, ROWS), F32),
            pltpu.VMEM((2 * RING * 4, 1, ROWS), F32),
            pltpu.VMEM((DIM, ROWS), F32),
            pltpu.VMEM((DIM, ROWS), F32),
            pltpu.VMEM((1, DIM), jnp.int32),
            pltpu.SMEM((1, DIM), jnp.int32),
            pltpu.VMEM((RING, 2, PB, wide), F32),
            pltpu.VMEM((RING, 2, PB, wide), F32),
            pltpu.VMEM((RING, 2, PB, wide), F32),
            pltpu.VMEM((2, 7, PB, wide), BF16),
            pltpu.VMEM((2, 7, PB, wide), BF16),
            pltpu.VMEM((2, RING, 16, DIM), BF16),
            pltpu.VMEM((4 * RING, 16, DIM), BF16),
            pltpu.VMEM((RING, 16, DIM), BF16),
            pltpu.VMEM((RING, 2, 2, RB, DIM), F32),
            pltpu.VMEM((2, HALF, 2, 2, RB, DIM), BF16),
            pltpu.VMEM((2, HALF, 2, 2, RB, DIM), BF16),
            pltpu.VMEM((2, 2, RB, DIM), F32),
            pltpu.VMEM((2, RB, DIM), BF16),
            pltpu.VMEM((2, RB, DIM), BF16),
            dma((7,)),
            dma,
            dma((RING * 2,)),
            dma((RING,)),
            dma,
            dma((GROUP,)),
            dma,
            dma((GROUP,)),
            dma,
            dma,
            dma((RING,)),
            dma,
            dma((2, 7)),
            dma,
            dma,
            dma,
            dma,
            dma((2,)),
            dma((2, HALF, 2)),
            dma,
            dma((2,)),
            pltpu.SemaphoreType.REGULAR,
        ],
        compiler_params=pltpu.CompilerParams(
            collective_id=0, has_side_effects=True, vmem_limit_bytes=VMEM
        ),
        name="attention_backward",
    )(
        query[0], resp_key[0], resp_value[0], prompt_key, prompt_value,
        saved_out[0], out_grad[0], resp_len, prompt_order[None],
    )
    outs = pl.pallas_call(
        hand_over,
        out_shape=tuple(jax.ShapeDtypeStruct(out.shape, out.dtype) for out in outs),
        in_specs=[vmem] * 5,
        out_specs=(vmem,) * 5,
        compiler_params=pltpu.CompilerParams(vmem_limit_bytes=VMEM),
        name="hand_over",
    )(*outs)
    return (outs[0][None], outs[1][None], outs[2][None], outs[3], outs[4])


def solution(mesh):
    token = P("resp", "ctx", None)
    block = P("resp", None)
    return jax.shard_map(
        local,
        mesh=mesh,
        in_specs=(token, token, token, block, block, token, token, P("resp"), P()),
        out_specs=(token, token, token, block, block),
        check_vma=False,
    )
```

time: 82 us -> 70 us (0.85)
  the two profiles are of different devices: /device:TPU:4 before, /device:TPU:8 now
where the time goes in v2:
time: 70 us; the launch traced here: 69.8 us
  Pallas kernels  68.5 us (98%)
  between operations  1.29 us (2%)
    pallas_call x1, Pallas kernels, local(): pl.pallas_call(body, out_shape=(jax.ShapeDtypeStruct((TOKENS, HEADS * DIM...  66.8 us
    pallas_call x1, Pallas kernels, local(): pl.pallas_call(hand_over, out_shape=tuple((jax.ShapeDtypeStruct(out.shape...  1.72 us

profile of v2, /device:TPU:8, one launch (start us, length us, event | category | flops | bytes accessed | tf_op | source)
XLA Modules:
  0.0 69.8 jit_solution(13749216577173756893)
XLA Ops:
  1.3 66.8 %attention_backward.1 = (bf16[128,1024]{1,0:T(8,128)(2,1)}, bf16[128,128]{1,0:T(8,128)(2,1)}, bf16[128,128]{1,0:T(8,128)(2,1)}, bf16[64,128]{1,0:T(8,128)(2,1)}, bf16[64,128]{1,0:T(8,128)(2,1)}) custom-call(bf16[128,1024]{1,0:T(8,128)(2,1)} %bitcast.9, bf16[128,128]{1,0:T(8,128)(2,1)} %bitcast.12, bf16[128,128]{1,0:T(8,128)(2,1)} %bitcast.13, ...), custom_call_target="tpu_custom_call" | custom-call | tf_op jit(solution)/shard_map/attention_backward/pallas_call | solution.py:549
  68.1 1.7 %hand_over.1 = (bf16[128,1024]{1,0:T(8,128)(2,1)}, bf16[128,128]{1,0:T(8,128)(2,1)}, bf16[128,128]{1,0:T(8,128)(2,1)}, bf16[64,128]{1,0:T(8,128)(2,1)}, bf16[64,128]{1,0:T(8,128)(2,1)}) custom-call(bf16[128,1024]{1,0:T(8,128)(2,1)} %get-tuple-element.15.refs_0_, bf16[128,128]{1,0:T(8,128)(2,1)} %get-tuple-element.16.refs_1_, ...), custom_call_target="tpu_custom_call" | custom-call | tf_op jit(solution)/shard_map/hand_over/pallas_call | solution.py:628

commit v3 on v2

--- a/solution.py
+++ b/solution.py
@@ -114,8 +114,8 @@
         return remote(slot(b), slot(b), ss, rs(b), device)
 
     def arrived(ring, b):
-        slot, _, rs, ss, at = ring
-        remote(slot(b), slot(b), ss, rs(b), at(1)).wait_recv()
+        slot, _, rs, ss, _ = ring
+        remote(slot(b), slot(b), ss, rs(b), other_core).wait_recv()
 
     def core_copy(s, own):
         b = a_block(s, own)
@@ -141,23 +141,23 @@
         def _():
             ring_copy(ring, s, own, ring[4](-1)).start()
 
-    def ring_step(ring, s, core_too):
-        for own in (True, False):
-            arrived(ring, ring[1](s, own))
-            hops(ring, s, own)
-            if core_too:
-                core_copy(s, own).start()
-
-    def first_copies(ring, pair):
+    def ring_step(ring, s, own):
+        arrived(ring, ring[1](s, own))
+        hops(ring, s, own)
+        if ring is ring_a:
+            core_copy(s, own).start()
+
+    for across in (False, True):
+        for ring in (ring_a, ring_k):
+            for step in (1, -1):
+                ring_copy(ring, 0, True, ring[4](step, across)).start()
+    core_copy(0, True).start()
+    ring_copy(ring_a, 0, True, mirror).start()
+    ring_copy(ring_k, 0, True, x_pair).start()
+    for across in (False, True):
         for step in (1, -1):
-            for across in (False, True):
-                ring_copy(ring, 0, True, ring[4](step, across)).start()
-        ring_copy(ring, 0, True, pair).start()
-
-    first_copies(ring_a, mirror)
-    core_copy(0, True).start()
-    first_copies(ring_k, x_pair)
-    first_copies(ring_v, x_pair)
+            ring_copy(ring_v, 0, True, at_y(step, across)).start()
+    ring_copy(ring_v, 0, True, x_pair).start()
 
     def prepare(h):
         lanes = slice(h * DIM, (h + 1) * DIM)
@@ -229,8 +229,9 @@
                 then(s)
 
     def first(k, _):
-        both_sides(k, lambda s: ring_step(ring_a, s, True))
-        both_sides(k, lambda s: ring_step(ring_k, s, False))
+        for own in (True, False):
+            for ring in (ring_a, ring_k):
+                both_sides(k + 1, lambda s: ring_step(ring, s, own))
 
         def prompt_side(s, _):
             @pl.when((s >= 0) & (s < RING))
@@ -242,7 +243,8 @@
             return 0
 
         lax.fori_loop(2 * k - 1, 2 * k + 1, prompt_side, 0)
-        both_sides(k - 1, lambda s: ring_step(ring_v, s, False))
+        for own in (True, False):
+            both_sides(k + 1, lambda s: ring_step(ring_v, s, own))
 
         def resp_side(s, _):
             lev = level_at(s, y)
@@ -258,6 +260,7 @@
         return 0
 
     lax.fori_loop(0, HALF + 1, first, 0)
+    arrived(ring_v, b_block(0, False))
     inv_copy.wait()
     pl.semaphore_signal(token, inc=1, device_id=mirror, device_id_type=MESH)
 
@@ -406,6 +409,28 @@
                     d_send[d, j - 1, kv, sub] = value.astype(BF16)
                 d_copy(j, kv, up).start()
 
+    def resp_level(s):
+        lev = level_at(s, y)
+
+        @pl.when(lev <= y)
+        def _():
+            keys = rkeys[level_rows(lev), :]
+            dp = jnp.dot(rvalues[level_rows(lev), :], dot[...], preferred_element_type=F32)
+            block = (RING + lev) * 4
+            p = pst[pl.ds(block, 4)].reshape(CHUNK, ROWS) * fac[block]
+            g = (p * (dp - delta[...])).astype(BF16)
+            dv = jnp.dot(p.astype(BF16), dos[...], preferred_element_type=F32)
+            dk = jnp.dot(g, qs[...], preferred_element_type=F32) * SCALE
+            dqr[...] += jnp.dot(keys.T, g, preferred_element_type=F32)
+            for sub in range(2):
+                rows = slice(sub * RB, (sub + 1) * RB)
+                d_own[lev, 0, sub] = dk[rows]
+                d_own[lev, 1, sub] = dv[rows]
+
+        @pl.when(lev > y)
+        def _():
+            d_own[lev] = jnp.zeros((2, 2, RB, DIM), F32)
+
     def prompt_second(i, _):
         s = RING - 1 - i
         lev = level_at(s, z)
@@ -438,54 +463,37 @@
             def _():
                 c_events(when)
 
+        @pl.when(s == 5)
+        def _():
+            resp_level(RING - 1)
+            d_step(1)
+
         return 0
 
     lax.fori_loop(0, RING, prompt_second, 0)
-    arrived(ring_v, b_block(0, False))
-    ring_step(ring_v, jnp.int32(RING - 1), False)
+    c_message(3, True)
+    c_message(3, False)
 
     def resp_second(i, _):
-        s = RING - 1 - i
-        lev = level_at(s, y)
-
-        @pl.when(lev <= y)
-        def _():
-            keys = rkeys[level_rows(lev), :]
-            dp = jnp.dot(rvalues[level_rows(lev), :], dot[...], preferred_element_type=F32)
-            block = (RING + lev) * 4
-            p = pst[pl.ds(block, 4)].reshape(CHUNK, ROWS) * fac[block]
-            g = (p * (dp - delta[...])).astype(BF16)
-            dv = jnp.dot(p.astype(BF16), dos[...], preferred_element_type=F32)
-            dk = jnp.dot(g, qs[...], preferred_element_type=F32) * SCALE
-            dqr[...] += jnp.dot(keys.T, g, preferred_element_type=F32)
-            for sub in range(2):
-                rows = slice(sub * RB, (sub + 1) * RB)
-                d_own[lev, 0, sub] = dk[rows]
-                d_own[lev, 1, sub] = dv[rows]
-
-        @pl.when(lev > y)
-        def _():
-            d_own[lev] = jnp.zeros((2, 2, RB, DIM), F32)
-
-        @pl.when(s == 7)
-        def _():
-            d_step(1)
-            c_message(3, True)
-            c_message(3, False)
+        s = RING - 2 - i
+        resp_level(s)
 
         @pl.when(s == 6)
         def _():
             c_message(6, True)
             c_message(6, False)
 
+        @pl.when(s == 5)
+        def _():
+            d_step(2)
+
         @pl.when(s == 3)
         def _():
             c_scatter()
-            d_step(2)
 
         return 0
 
-    lax.fori_loop(0, RING, resp_second, 0)
+    lax.fori_loop(0, RING - 1, resp_second, 0)
 
     dq_factor = jnp.exp2(m_dq[...] - m_all) * inv_l
     for h in range(HEADS):
@@ -495,8 +503,8 @@
 
     d_step(3)
 
+    d_step(4)
     c_gather()
-    d_step(4)
 
     for kv in range(2):
         for up in (True, False):

time: 70 us -> 67 us (0.957)
  Pallas kernels: 68.5 us -> 65.5 us
    pallas_call x1, Pallas kernels: 66.8 us -> 63.8 us  [local(): pl.pallas_call(body, out_shape=(jax.ShapeDtypeStruct((TOKENS, HEADS * DIM...]
where the time goes in v3:
time: 67 us; the launch traced here: 66.8 us
  Pallas kernels  65.5 us (98%)
  between operations  1.29 us (2%)
    pallas_call x1, Pallas kernels, local(): pl.pallas_call(body, out_shape=(jax.ShapeDtypeStruct((TOKENS, HEADS * DIM...  63.8 us
    pallas_call x1, Pallas kernels, local(): pl.pallas_call(hand_over, out_shape=tuple((jax.ShapeDtypeStruct(out.shape...  1.72 us

profile of v3, /device:TPU:8, one launch (start us, length us, event | category | flops | bytes accessed | tf_op | source)
XLA Modules:
  0.0 66.8 jit_solution(7452581201134771147)
XLA Ops:
  1.3 63.8 %attention_backward.1 = (bf16[128,1024]{1,0:T(8,128)(2,1)}, bf16[128,128]{1,0:T(8,128)(2,1)}, bf16[128,128]{1,0:T(8,128)(2,1)}, bf16[64,128]{1,0:T(8,128)(2,1)}, bf16[64,128]{1,0:T(8,128)(2,1)}) custom-call(bf16[128,1024]{1,0:T(8,128)(2,1)} %bitcast.9, bf16[128,128]{1,0:T(8,128)(2,1)} %bitcast.12, bf16[128,128]{1,0:T(8,128)(2,1)} %bitcast.13, ...), custom_call_target="tpu_custom_call" | custom-call | tf_op jit(solution)/shard_map/attention_backward/pallas_call | solution.py:557
  65.1 1.7 %hand_over.1 = (bf16[128,1024]{1,0:T(8,128)(2,1)}, bf16[128,128]{1,0:T(8,128)(2,1)}, bf16[128,128]{1,0:T(8,128)(2,1)}, bf16[64,128]{1,0:T(8,128)(2,1)}, bf16[64,128]{1,0:T(8,128)(2,1)}) custom-call(bf16[128,1024]{1,0:T(8,128)(2,1)} %get-tuple-element.15.refs_0_, bf16[128,128]{1,0:T(8,128)(2,1)} %get-tuple-element.16.refs_1_, ...), custom_call_target="tpu_custom_call" | custom-call | tf_op jit(solution)/shard_map/hand_over/pallas_call | solution.py:636

commit v4 on v3

--- a/solution.py
+++ b/solution.py
@@ -21,7 +21,7 @@
 CHUNK = 256
 TOKENS = 128
 ROWS = TOKENS * HEADS
-VMEM = 56 * 1024 * 1024
+VMEM = 48 * 1024 * 1024
 F32 = jnp.float32
 BF16 = jnp.bfloat16
 
@@ -33,9 +33,9 @@
 
 
 def body(
-    q_hbm, rk_hbm, rv_hbm, pk_hbm, pv_hbm, o_hbm, do_hbm, len_ref, order_ref,
+    q_hbm, rk_hbm, rv_hbm, pk_hbm, pv_hbm, o_hbm, do_hbm, len_ref, order_hbm,
     dq_ref, rdk_ref, rdv_ref, pdk_ref, pdv_ref,
-    q_ref, o_ref, do_ref, pkv, rkeys, rvalues, qs, dos, qt, dot, delta, pst, gst, mst, m_run, m_dq, l_run, fac, dqt, dqr, inv_v, inv,
+    order_ref, q_ref, o_ref, do_ref, pkv, rkeys, rvalues, qs, dos, qt, dot, delta, pst, gst, mst, m_run, m_dq, l_run, fac, dqt, dqr, inv_v, inv,
     c1_own, c1_send, c1_recv, c2_send, c2_recv,
     rs_send, rs_recv, ag_recv,
     d_own, d_send, d_recv, d_tot, d_xsend, d_xrecv,
@@ -80,7 +80,7 @@
     moves = (
         (pk_hbm, pkv.at[p_rows, 0:DIM]), (pv_hbm, pkv.at[p_rows, DIM : 2 * DIM]),
         (rk_hbm, rkeys.at[r_rows]), (rv_hbm, rvalues.at[r_rows]),
-        (q_hbm, q_ref), (do_hbm, do_ref), (o_hbm, o_ref),
+        (q_hbm, q_ref), (do_hbm, do_ref), (o_hbm, o_ref), (order_hbm, order_ref),
     )
     reads = [pltpu.make_async_copy(src, dst, in_s.at[i]) for i, (src, dst) in enumerate(moves)]
     for read in reads:
@@ -563,9 +563,10 @@
             jax.ShapeDtypeStruct((PB, DIM), BF16),
             jax.ShapeDtypeStruct((PB, DIM), BF16),
         ),
-        in_specs=[pl.BlockSpec(memory_space=pl.ANY)] * 7 + [smem, vmem],
+        in_specs=[pl.BlockSpec(memory_space=pltpu.HBM)] * 7 + [smem, pl.BlockSpec(memory_space=pltpu.HBM)],
         out_specs=(vmem,) * 5,
         scratch_shapes=[
+            pltpu.VMEM((1, RING * 4), jnp.int32),
             pltpu.VMEM((TOKENS, ROWS), BF16),
             pltpu.VMEM((TOKENS, ROWS), BF16),
             pltpu.VMEM((TOKENS, ROWS), BF16),
@@ -602,7 +603,7 @@
             pltpu.VMEM((2, 2, RB, DIM), F32),
             pltpu.VMEM((2, RB, DIM), BF16),
             pltpu.VMEM((2, RB, DIM), BF16),
-            dma((7,)),
+            dma((8,)),
             dma,
             dma((RING * 2,)),
             dma((RING,)),
@@ -630,8 +631,10 @@
         ),
         name="attention_backward",
     )(
-        query[0], resp_key[0], resp_value[0], prompt_key, prompt_value,
-        saved_out[0], out_grad[0], resp_len, prompt_order[None],
+        *(pltpu.with_memory_space_constraint(x, pltpu.HBM) for x in (
+            query[0], resp_key[0], resp_value[0], prompt_key, prompt_value, saved_out[0], out_grad[0],
+        )),
+        resp_len, pltpu.with_memory_space_constraint(prompt_order[None], pltpu.HBM),
     )
     outs = pl.pallas_call(
         hand_over,

time: 67 us -> 64.7 us (0.966)
  Pallas kernels: 65.5 us -> 63.2 us
    pallas_call x1, Pallas kernels: 63.8 us -> 62.4 us  [local(): pl.pallas_call(body, out_shape=(jax.ShapeDtypeStruct((TOKENS, HEADS * DIM...]
    pallas_call x1, Pallas kernels: 1.72 us -> 0.75 us  [local(): pl.pallas_call(hand_over, out_shape=tuple((jax.ShapeDtypeStruct(out.shape...]
where the time goes in v4:
time: 64.7 us; the launch traced here: 64.4 us
  Pallas kernels  63.2 us (98%)
  between operations  1.29 us (2%)
    pallas_call x1, Pallas kernels, local(): pl.pallas_call(body, out_shape=(jax.ShapeDtypeStruct((TOKENS, HEADS * DIM...  62.4 us

profile of v4, /device:TPU:8, one launch (start us, length us, event | category | flops | bytes accessed | tf_op | source)
XLA Modules:
  0.0 64.4 jit_solution(14840310178615331193)
XLA Ops:
  1.3 62.4 %attention_backward.1 = (bf16[128,1024]{1,0:T(8,128)(2,1)S(1)}, bf16[128,128]{1,0:T(8,128)(2,1)S(1)}, bf16[128,128]{1,0:T(8,128)(2,1)S(1)}, bf16[64,128]{1,0:T(8,128)(2,1)S(1)}, bf16[64,128]{1,0:T(8,128)(2,1)S(1)}) custom-call(bf16[128,1024]{1,0:T(8,128)(2,1)} %bitcast.9, bf16[128,128]{1,0:T(8,128)(2,1)} %bitcast.12, bf16[128,128]{1,0:T(8,128)(2,1)} %bitcast.13, ...), custom_call_target="tpu_custom_call" | custom-call | tf_op jit(solution)/shard_map/attention_backward/pallas_call | solution.py:557
  63.7 0.7 %hand_over.1 = (bf16[128,1024]{1,0:T(8,128)(2,1)}, bf16[128,128]{1,0:T(8,128)(2,1)}, bf16[128,128]{1,0:T(8,128)(2,1)}, bf16[64,128]{1,0:T(8,128)(2,1)}, bf16[64,128]{1,0:T(8,128)(2,1)}) custom-call(bf16[128,1024]{1,0:T(8,128)(2,1)S(1)} %get-tuple-element.15.refs_0_, bf16[128,128]{1,0:T(8,128)(2,1)S(1)} %get-tuple-element.16.refs_1_, ...), custom_call_target="tpu_custom_call" | custom-call | tf_op jit(solution)/shard_map/hand_over/pallas_call | solution.py:639
